TPU v7x, 32 devices: a whole 2x2x4 slice. The times are simulated.
32 devices in a mesh: rows: 16 (over z, y, x), cols: 2 (over core).
Axes of the slice: x: 2, y: 2, z: 4, core: 2. Of those that a mesh axis runs over, the one named last changes fastest.
Arguments:
- deviations: float32 [12288, 8192], P('rows', 'cols')
- test_signs: int32 [8192, 128], P('cols'), may hold values from -1 to 1, as said below
Outputs:
- basis: float32 [12288, 128], P('rows')
- projected: float32 [128, 8192], P('rows', 'cols')
Inputs may be any that keep to these rules, and one draw needn't show every extreme that they name: `test_signs`: every entry is -1 or 1.
All inputs are finite; a program needn't handle non-finite values.
Results may differ from a plain program's by a relative error of at most 0.0003.
Values sent between devices are 32-bit elements; how exact they have to be, the bound alone decides.
No kernel may reach another device: no remote copies, remote signals or barrier semaphores. Data moves between devices by JAX's collectives and lax.ppermute only.
A program may use at most 64 MiB of HBM per device.

v0:
```python
import math

import jax
import jax.numpy as jnp
from jax import lax
from jax.sharding import PartitionSpec as P

SCANS = 8192


precise = lax.Precision.HIGHEST


def gram_of(tall_block):
    return lax.dot_general(
        tall_block,
        tall_block,
        (((0,), (0,)), ((), ())),
        precision=precise,
        preferred_element_type=jnp.float32,
    )


def orthogonalize(tall_block, gram_sum):
    tri_low = jnp.linalg.cholesky(gram_sum)
    result = jax.scipy.linalg.solve_triangular(tri_low, tall_block.T, lower=True).T
    return (result, tri_low.T)


def one_pass(tall_block, total_of):
    return orthogonalize(tall_block, total_of(gram_of(tall_block)))[0]


def rows_first(gram_part):
    return lax.psum(gram_part, "rows")


def local(deviations, test_signs):
    test_matrix = test_signs.astype(jnp.float32) / math.sqrt(SCANS)
    samples = deviations.shape[0] * lax.axis_size("rows")
    sketch = lax.psum(
        jnp.dot(deviations, test_matrix, precision=precise, preferred_element_type=jnp.float32),
        "cols",
    )
    orthonormal = one_pass(sketch, rows_first)
    projected = lax.psum_scatter(
        lax.dot_general(
            orthonormal,
            deviations,
            (((0,), (0,)), ((), ())),
            precision=precise,
            preferred_element_type=jnp.float32,
        ),
        "rows",
        scatter_dimension=0,
        tiled=True,
    )
    return (orthonormal * math.sqrt(samples), projected)


def solution(mesh):
    return jax.shard_map(
        local,
        mesh=mesh,
        in_specs=(P("rows", "cols"), P("cols", None)),
        out_specs=(P("rows", None), P("rows", "cols")),
        check_vma=False,
    )
```

profile of v0, /device:TPU:0, one launch (start us, length us, event | category | flops | bytes accessed | tf_op | source)
XLA Modules:
  0.0 278.2 jit_solution(15051873100276450948)
XLA Ops:
  7.2 0.0 all-reduce.3.cloned.1.call-start
  7.2 16.5 %fusion.3 = f32[768,128]{0,1:T(8,128)} fusion(f32[768,4096]{1,0:T(8,128)} %param.2, s32[4096,128]{1,0:T(8,128)} %param.3), kind=kOutput, calls=%fused_computation.3 | convolution fusion | flops 4832886784 | bytes 15073280 | tf_op jit(solution)/shard_map/dot_general | solution.py:42
  23.7 0.0 all-reduce.3.cloned.1.call-update
  23.7 0.0 all-reduce.5.cloned.1.call-start
  23.8 21.3 %all-reduce.3.cloned.1.call-done = f32[768,128]{0,1:T(8,128)} async-done(((f32[768,128]{0,1:T(8,128)}), f32[768,128]{0,1:T(8,128)}) %all-reduce.3.cloned.1.call-update) | async-done | bytes 393232 | tf_op jit(solution)/shard_map/psum | solution.py:41
  45.1 2.2 fusion.12
  47.3 0.0 all-reduce.5.cloned.1.call-update
  47.3 0.2 reduce-scatter.2.cloned.1.call-start
  47.5 107.6 %all-reduce.5.cloned.1.call-done = f32[128,128]{0,1:T(8,128)} async-done(((f32[128,128]{0,1:T(8,128)}), f32[128,128]{0,1:T(8,128)}) %all-reduce.5.cloned.1.call-update) | async-done | bytes 65552 | tf_op jit(solution)/shard_map/psum | solution.py:35
  155.2 0.9 copy.5
  156.1 0.9 fusion.10
  157.0 11.7 %cholesky.16 = f32[128,128]{1,0:T(8,128)S(1)} custom-call(f32[128,128]{1,0:T(8,128)S(1)} %fusion.10), custom_call_target="Cholesky" | custom-call | tf_op jit(solution)/shard_map/jit(cholesky)/cholesky | solution.py:25
  168.7 0.6 compare_reduce_fusion
  169.3 0.7 fusion.7
  170.0 9.8 %custom-call.7 = f32[1,128,128]{1,2,0:T(8,128)S(1)} custom-call(f32[1,128,128]{2,1,0:T(8,128)S(1)} %fusion.7), custom_call_target="InvertDiagBlocksLowerTriangular" | custom-call | tf_op jit(solution)/shard_map/jit(_solve_triangular)/triangular_solve | solution.py:26
  179.8 1.5 fusion.8
  181.4 10.6 %fusion.13 = f32[128,4096]{1,0:T(8,128)} fusion(f32[128,768]{1,0:T(8,128)S(1)} %fusion.8, f32[768,4096]{1,0:T(8,128)} %param.2), kind=kOutput, calls=%fused_computation.18 | convolution fusion | flops 4831838208 | bytes 15073280 | tf_op jit(solution)/shard_map/dot_general | solution.py:47
  191.9 0.0 reduce-scatter.2.cloned.1.call-update
  192.0 0.9 copy.6
  192.9 78.8 %reduce-scatter.2.cloned.1.call-done = f32[8,4096]{1,0:T(8,128)} async-done(((f32[128,4096]{1,0:T(8,128)}), f32[8,4096]{1,0:T(8,128)}) %reduce-scatter.2.cloned.1.call-update) | async-done | bytes 131088 | tf_op jit(solution)/shard_map/reduce_scatter | solution.py:46
  (2 shorter events, 0.1 us)
Async XLA Ops:
  7.2 37.9 %all-reduce.3.cloned.1.call-start = ((), (), s32[]{:S(2)}) async-start(), calls=%async_computation.1 | async-start | bytes 786432 | tf_op jit(solution)/shard_map/psum | solution.py:41
  23.7 131.4 %all-reduce.5.cloned.1.call-start = ((), (), s32[]{:S(2)}) async-start(), calls=%async_computation.2 | async-start | bytes 131072 | tf_op jit(solution)/shard_map/psum | solution.py:35
  47.3 224.4 %reduce-scatter.2.cloned.1.call-start = ((), (), s32[]{:S(2)}) async-start(), calls=%async_computation.3 | async-start | bytes 2228224 | tf_op jit(solution)/shard_map/reduce_scatter | solution.py:46
Sparse Core Ops, SparseCore 0:
  23.8 21.1 all-reduce.2
  52.0 103.0 all-reduce.4
  192.1 79.5 reduce-scatter.1
where the time goes:
time: 279 us; the launch traced here: 278 us
  waiting for transfers between devices  208 us (75%)
  matrix products  30.8 us (11%)
  other arithmetic  23.7 us (8%)
  between operations  13.8 us (5%)
    psum x1, waiting for transfers between devices, rows_first(): return lax.psum(gram_part, 'rows')  108 us
    reduce_scatter x1, waiting for transfers between devices, local(): lax.psum_scatter(lax.dot_general(orthonormal, deviations, (((0,), (0,)),...  78.8 us
    psum x1, waiting for transfers between devices, local(): lax.psum(jnp.dot(deviations, test_matrix, precision=precise, preferred_el...  21.3 us
    dot_general x1, matrix products, local(): jnp.dot(deviations, test_matrix, precision=precise, preferred_element_typ...  16.5 us
    another operation x3, other arithmetic, orthogonalize(): tri_low = jnp.linalg.cholesky(gram_sum)  12.4 us
    dot_general x1, matrix products, local(): lax.dot_general(orthonormal, deviations, (((0,), (0,)), ((), ())), precis...  10.6 us
    another operation x2, other arithmetic, orthogonalize(): jax.scipy.linalg.solve_triangular(tri_low, tall_block.T, lower=True)  10.5 us
  transfers between devices with their start and end apart: 3, of which 3 were waited for; matrix products, arithmetic and copies ran while one was open for 0% of the time, Pallas kernels for 0%

commit v1 on v0

v1 whole, which is shorter than its diff:
```python
import functools
import math

import jax
import jax.numpy as jnp
from jax import lax
from jax.experimental import pallas as pl
from jax.experimental.pallas import tpu as pltpu
from jax.sharding import PartitionSpec as P

SCANS = 8192

precise = lax.Precision.HIGHEST
MIB = 1 << 20


def split(value):
    high = value.astype(jnp.bfloat16)
    low = (value - high.astype(jnp.float32)).astype(jnp.bfloat16)
    return high, low


def dot(a, b):
    return jnp.dot(a, b, preferred_element_type=jnp.float32)


def vmem():
    return pl.BlockSpec(memory_space=pltpu.VMEM)


def params(mib=40):
    return pltpu.CompilerParams(vmem_limit_bytes=mib * MIB)


def sketch_kernel(unit, gain, dev_ref, sign_ref, out_ref):
    step = pl.program_id(0)
    omega = (sign_ref[...].astype(jnp.float32) * unit).astype(jnp.bfloat16)
    high, low = split(dev_ref[...])
    part = dot(high, omega) + dot(low, omega)

    @pl.when(step == 0)
    def _():
        out_ref[...] = part

    @pl.when(step > 0)
    def _():
        out_ref[...] += part

    @pl.when(step == pl.num_programs(0) - 1)
    def _():
        out_ref[...] *= gain


def sketch_of(dev, signs):
    rows, cols = dev.shape
    rank = signs.shape[1]
    block = min(512, cols)
    unit = 2.0 ** -math.ceil(math.log2(math.sqrt(SCANS)))
    gain = 1.0 / (math.sqrt(SCANS) * unit)
    return pl.pallas_call(
        functools.partial(sketch_kernel, unit, gain),
        grid=(cols // block,),
        in_specs=[
            pl.BlockSpec((rows, block), lambda i: (0, i)),
            pl.BlockSpec((block, rank), lambda i: (i, 0)),
        ],
        out_specs=pl.BlockSpec((rows, rank), lambda i: (0, 0)),
        out_shape=jax.ShapeDtypeStruct((rows, rank), jnp.float32),
        compiler_params=params(),
    )(dev, signs)


def gram_kernel(parts, *refs):
    total_ref, pair_ref, gram_ref = refs[parts:]
    total = refs[0][...]
    for ref in refs[1:parts]:
        total = total + ref[...]
    total_ref[...] = total
    flat = total.T
    high, low = split(flat)
    rank = flat.shape[0]
    pair_ref[:rank, :] = high
    pair_ref[rank:, :] = low
    gram_ref[...] = lax.dot_general(
        flat, total, (((1,), (0,)), ((), ())),
        precision=precise, preferred_element_type=jnp.float32,
    )


def gram_of(*sketches):
    rows, rank = sketches[0].shape
    return pl.pallas_call(
        functools.partial(gram_kernel, len(sketches)),
        in_specs=[vmem()] * len(sketches),
        out_specs=[vmem()] * 3,
        out_shape=[
            jax.ShapeDtypeStruct((rows, rank), jnp.float32),
            jax.ShapeDtypeStruct((2 * rank, rows), jnp.bfloat16),
            jax.ShapeDtypeStruct((rank, rank), jnp.float32),
        ],
        compiler_params=params(),
    )(*sketches)


def cross_kernel(steps, index_ref, pair_ref, dev_ref, first_ref, second_ref):
    step = pl.program_id(0)
    rank = first_ref.shape[0]
    high, low = split(dev_ref[...])
    both = dot(pair_ref[...], high)
    value = (both[:rank] + both[rank:]) + dot(pair_ref[:rank, :], low)

    @pl.when(step < steps)
    def _():
        first_ref[...] = value

    @pl.when(step >= steps)
    def _():
        second_ref[...] = value


def cross_of(index, pair, dev, width):
    rank, rows = pair.shape[0] // 2, pair.shape[1]
    block = min(512, width)
    steps = width // block

    def dev_map(i, index_ref):
        return (0, index_ref[i // steps] * steps + i % steps)

    return pl.pallas_call(
        functools.partial(cross_kernel, steps),
        grid_spec=pltpu.PrefetchScalarGridSpec(
            num_scalar_prefetch=1,
            grid=(2 * steps,),
            in_specs=[
                pl.BlockSpec((2 * rank, rows), lambda i, index_ref: (0, 0)),
                pl.BlockSpec((rows, block), dev_map),
            ],
            out_specs=[
                pl.BlockSpec((rank, block), lambda i, index_ref: (0, jnp.minimum(i, steps - 1))),
                pl.BlockSpec((rank, block), lambda i, index_ref: (0, jnp.maximum(i - steps, 0))),
            ],
        ),
        out_shape=[jax.ShapeDtypeStruct((rank, width), jnp.float32)] * 2,
        compiler_params=params(),
    )(index, pair, dev)


def project_kernel(groups, index_ref, inverse_ref, a_ref, b_ref, c_ref, d_ref, *outs):
    group = outs[0].shape[0]
    half = a_ref.shape[1]
    left = a_ref[...] + b_ref[...]
    right = c_ref[...] + d_ref[...]
    for k in range(groups):
        start = pl.multiple_of((index_ref[0] ^ k) * group, group)
        factor = inverse_ref[pl.ds(start, group), :]
        outs[k][:, :half] = jnp.dot(factor, left, precision=precise, preferred_element_type=jnp.float32)
        outs[k][:, half:] = jnp.dot(factor, right, precision=precise, preferred_element_type=jnp.float32)


def project(index, inverse, parts, groups):
    rank, half = parts[0].shape
    shape = jax.ShapeDtypeStruct((rank // groups, 2 * half), jnp.float32)
    return pl.pallas_call(
        functools.partial(project_kernel, groups),
        in_specs=[pl.BlockSpec(memory_space=pltpu.SMEM)] + [vmem()] * 5,
        out_specs=[vmem()] * groups,
        out_shape=[shape] * groups,
        compiler_params=params(),
    )(index, inverse, *parts)


def local(deviations, test_signs):
    rows, cols = deviations.shape
    n, n_cols = lax.axis_size("rows"), lax.axis_size("cols")
    samples = rows * n
    me = lax.axis_index("rows")
    x, y, z = me & 1, (me >> 1) & 1, me >> 2
    n_z = n // 4

    def swap(value, bit):
        return lax.ppermute(value, "rows", [(i, i ^ bit) for i in range(n)])

    part = sketch_of(deviations, test_signs)
    step = 1
    while 2 * step < n_cols:
        part = part + lax.ppermute(part, "cols", [(i, i ^ step) for i in range(n_cols)])
        step *= 2
    other = lax.ppermute(part, "cols", [(i, i ^ step) for i in range(n_cols)])
    sketch, pair, gram = gram_of(part, other)

    step = 1
    while step < n:
        gram = gram + swap(gram, step)
        step *= 2

    width = cols // 4
    away = jnp.stack([1 - x, 3 - y]).astype(jnp.int32)
    home = jnp.stack([x, 2 + y]).astype(jnp.int32)
    send_x, send_y = cross_of(away, pair, deviations, width)
    got_x, got_y = swap(send_x, 1), swap(send_y, 2)
    keep_x, keep_y = cross_of(home, pair, deviations, width)
    half = width // 2

    def cut(value, which):
        return lax.dynamic_slice_in_dim(value, which * half, half, 1)

    next_x = cut(keep_x, 1 - y) + cut(got_x, 1 - y)
    next_y = cut(keep_y, 1 - x) + cut(got_y, 1 - x)
    last_x = cut(keep_x, y) + cut(got_x, y)
    last_y = cut(keep_y, x) + cut(got_y, x)
    then_x, then_y = swap(next_x, 2), swap(next_y, 1)

    low = jnp.linalg.cholesky(gram)
    inverse = jax.scipy.linalg.solve_triangular(low, jnp.eye(gram.shape[0], dtype=jnp.float32), lower=True)

    groups = project(z[None], inverse, (last_x, then_x, last_y, then_y), n_z)
    total = groups[0]
    for k in range(1, n_z):
        total = total + swap(groups[k], 4 * k)

    each = total.shape[0] // 4
    mine = me & 3
    found = []
    for k in range(4):
        block = lax.dynamic_slice_in_dim(total, (mine ^ k) * each, each, 0)
        found.append(swap(block, k) if k else block)
    for bit in (1, 2):
        flip = (mine & bit) != 0
        found = [jnp.where(flip, found[k ^ bit], found[k]) for k in range(4)]
    projected = jnp.concatenate(
        [found[k][:, :half] for k in (0, 2, 1, 3)] + [found[k][:, half:] for k in (0, 1, 2, 3)], axis=1
    )

    basis = lax.dot_general(
        sketch, inverse, (((1,), (1,)), ((), ())),
        precision=precise, preferred_element_type=jnp.float32,
    ) * math.sqrt(samples)
    return (basis, projected)


def solution(mesh):
    return jax.shard_map(
        local,
        mesh=mesh,
        in_specs=(P("rows", "cols"), P("cols", None)),
        out_specs=(P("rows", None), P("rows", "cols")),
        check_vma=False,
    )
```

time: 279 us -> 92 us (0.33)
  waiting for transfers between devices: 208 us -> 14.9 us
  matrix products: 30.8 us -> 1.47 us
  starting transfers between devices: 0.3 us -> 21.5 us
  Pallas kernels: 0 us -> 17.2 us
  between operations: 13.8 us -> 0.85 us
  local copies, waits for them, and re-layouts: 1.84 us -> 11.6 us
    psum x2 -> x0, waiting for transfers between devices: 129 us -> none  [the longest x1 108 us: rows_first(): return lax.psum(gram_part, 'rows')]
    reduce_scatter x1 -> x0, waiting for transfers between devices: 78.8 us -> none  [local(): lax.psum_scatter(lax.dot_general(orthonormal, deviations, (((0,), (0,)),...]
    dot_general x3 -> x1, matrix products: 29.3 us -> 1.22 us  [local(): lax.dot_general(sketch, inverse, (((1,), (1,)), ((), ())), precision=prec...]
    ppermute x0 -> x15, starting transfers between devices: none -> 21.5 us  [the longest x14 21 us: swap(): return lax.ppermute(value, 'rows', [(i, i ^ bit) for i in range(n)])]
    pallas_call x0 -> x5, Pallas kernels: none -> 17.2 us  [the longest x1 9.18 us: sketch_of(): pl.pallas_call(functools.partial(sketch_kernel, unit, gain), grid=(cols /...]
    ppermute x0 -> x15, waiting for transfers between devices: none -> 14.9 us  [the longest x14 13.5 us: swap(): return lax.ppermute(value, 'rows', [(i, i ^ bit) for i in range(n)])]
    unnamed x1 -> x15, local copies, waits for them, and re-layouts: 0.91 us -> 11.4 us
    another operation x5 -> x6, other arithmetic: 22.9 us -> 22.9 us  [the longest x3 12.4 us: local(): low = jnp.linalg.cholesky(gram)]
  transfers between devices with their start and end apart: 3 -> 15, of which waited for: 3 -> 8; matrix products, arithmetic and copies ran while one was open for 0% -> 28% of each run, Pallas kernels for 0% -> 7%
where the time goes in v1:
time: 92 us; the launch traced here: 91.7 us
  other arithmetic  24.2 us (26%)
  starting transfers between devices  21.5 us (23%)
  Pallas kernels  17.2 us (19%)
  waiting for transfers between devices  14.9 us (16%)
  local copies, waits for them, and re-layouts  11.6 us (13%)
  matrix products  1.47 us (2%)
    ppermute x14, starting transfers between devices, swap(): return lax.ppermute(value, 'rows', [(i, i ^ bit) for i in range(n)])  21 us
    ppermute x14, waiting for transfers between devices, swap(): return lax.ppermute(value, 'rows', [(i, i ^ bit) for i in range(n)])  13.5 us
    another operation x3, other arithmetic, local(): low = jnp.linalg.cholesky(gram)  12.4 us
    unnamed x15, local copies, waits for them, and re-layouts  11.4 us
    another operation x2, other arithmetic, local(): jax.scipy.linalg.solve_triangular(low, jnp.eye(gram.shape[0], dtype=jnp.f...  10.5 us
    pallas_call x1, Pallas kernels, sketch_of(): pl.pallas_call(functools.partial(sketch_kernel, unit, gain), grid=(cols /...  9.18 us
    pallas_call x2, Pallas kernels, cross_of(): pl.pallas_call(functools.partial(cross_kernel, steps), grid_spec=pltpu.Pr...  6.48 us
  transfers between devices with their start and end apart: 15, of which 8 were waited for; matrix products, arithmetic and copies ran while one was open for 28% of the time, Pallas kernels for 7%

profile of v1, /device:TPU:0, one launch (start us, length us, event | category | flops | bytes accessed | tf_op | source)
XLA Modules:
  0.0 91.7 jit_solution(11496488183225072621)
XLA Ops:
  0.6 1.6 %copy-done.2 = s32[4096,128]{1,0:T(8,128)S(1)} copy-done((s32[4096,128]{1,0:T(8,128)S(1)}, s32[4096,128]{1,0:T(8,128)}, u32[]{:S(2)}) %copy-start.2) | copy-done | bytes 2097176
  2.2 9.2 %shard_map.41.refs_0_ = f32[768,128]{1,0:T(8,128)S(1)} custom-call(f32[768,4096]{1,0:T(8,128)} %dev_ref.5, s32[4096,128]{1,0:T(8,128)S(1)} %copy-done.2), custom_call_target="tpu_custom_call" | custom-call | tf_op jit(solution)/shard_map/pallas_call | solution.py:60
  11.4 0.5 collective-permute-start
  11.9 1.3 %collective-permute-done.refs_1_ = f32[768,128]{1,0:T(8,128)S(1)} collective-permute-done((f32[768,128]{1,0:T(8,128)S(1)}, f32[768,128]{1,0:T(8,128)S(1)}, u32[]{:S(2)}, u32[]{:S(2)}) %collective-permute-start) | collective-permute-done | bytes 393248 | tf_op jit(solution)/shard_map/ppermute | solution.py:188
  13.3 0.5 shard_map.42
  13.8 0.1 copy.5
  13.9 2.9 %collective-permute-start.1 = (f32[128,128]{0,1:T(8,128)S(1)}, f32[128,128]{0,1:T(8,128)S(1)}, u32[]{:S(2)}, u32[]{:S(2)}) collective-permute-start(f32[128,128]{0,1:T(8,128)S(1)} %copy.5), channel_id=1, source_target_pairs={{0,2},{2,0},{4,6},{6,4},{8,10},{10,8},{12,14},{14,12},{16,18},{18,... | collective-permute-start | bytes 196616 | tf_op jit(solution)/shard_map/ppermute | solution.py:181
  16.8 2.4 %collective-permute-done.1 = f32[128,128]{0,1:T(8,128)S(1)} collective-permute-done((f32[128,128]{0,1:T(8,128)S(1)}, f32[128,128]{0,1:T(8,128)S(1)}, u32[]{:S(2)}, u32[]{:S(2)}) %collective-permute-start.1) | collective-permute-done | bytes 65568 | tf_op jit(solution)/shard_map/ppermute | solution.py:181
  19.3 2.0 %collective-permute-start.2 = (f32[128,128]{0,1:T(8,128)S(1)}, f32[128,128]{0,1:T(8,128)S(1)}, u32[]{:S(2)}, u32[]{:S(2)}) collective-permute-start(f32[128,128]{0,1:T(8,128)S(1)} %add.76), channel_id=1, source_target_pairs={{0,4},{2,6},{4,0},{6,2},{8,12},{10,14},{12,8},{14,10},{16,20},{18,... | collective-permute-start | bytes 196616 | tf_op jit(solution)/shard_map/ppermute | solution.py:181
  21.2 2.4 %collective-permute-done.2 = f32[128,128]{0,1:T(8,128)S(1)} collective-permute-done((f32[128,128]{0,1:T(8,128)S(1)}, f32[128,128]{0,1:T(8,128)S(1)}, u32[]{:S(2)}, u32[]{:S(2)}) %collective-permute-start.2) | collective-permute-done | bytes 65568 | tf_op jit(solution)/shard_map/ppermute | solution.py:181
  23.6 2.0 %collective-permute-start.3 = (f32[128,128]{0,1:T(8,128)S(1)}, f32[128,128]{0,1:T(8,128)S(1)}, u32[]{:S(2)}, u32[]{:S(2)}) collective-permute-start(f32[128,128]{0,1:T(8,128)S(1)} %add.77), channel_id=1, source_target_pairs={{0,8},{2,10},{4,12},{6,14},{8,0},{10,2},{12,4},{14,6},{16,24},{18,... | collective-permute-start | bytes 196616 | tf_op jit(solution)/shard_map/ppermute | solution.py:181
  25.6 0.1 pad_add_fusion
  25.7 4.6 %copy-done = f32[768,4096]{1,0:T(8,128)S(1)} copy-done((f32[768,4096]{1,0:T(8,128)S(1)}, f32[768,4096]{1,0:T(8,128)}, u32[]{:S(2)}) %copy-start) | copy-done | bytes 12582936
  30.3 3.2 %shard_map.44 = (f32[128,1024]{1,0:T(8,128)S(1)}, f32[128,1024]{1,0:T(8,128)S(1)}) custom-call(s32[2]{0:T(128)S(1)} %get-tuple-element.36.index_ref, bf16[256,768]{1,0:T(8,128)(2,1)S(1)} %get-tuple-element.15.pair_ref, f32[768,4096]{1,0:T(8,128)S(1)} %copy-done), custom_call_target="tpu_custom_call" | custom-call | tf_op jit(solution)/shard_map/pallas_call | solution.py:129
  33.5 1.6 %collective-permute-start.5 = (f32[128,1024]{1,0:T(8,128)S(1)}, f32[128,1024]{1,0:T(8,128)S(1)}, u32[]{:S(2)}, u32[]{:S(2)}) collective-permute-start(f32[128,1024]{1,0:T(8,128)S(1)} %get-tuple-element.17), channel_id=1, source_target_pairs={{0,2},{2,0},{4,6},{6,4},{8,10},{10,8},{12,14},{14,12},{16,18},{18,... | collective-permute-start | bytes 1572872 | tf_op jit(solution)/shard_map/ppermute | solution.py:181
  35.1 0.0 collective-permute-done.3
  35.1 2.7 %collective-permute-start.4 = (f32[128,128]{0,1:T(8,128)S(1)}, f32[128,128]{0,1:T(8,128)S(1)}, u32[]{:S(2)}, u32[]{:S(2)}) collective-permute-start(f32[128,128]{0,1:T(8,128)S(1)} %add.78), channel_id=1, source_target_pairs={{0,16},{2,18},{4,20},{6,22},{8,24},{10,26},{12,28},{14,30},{16,0},... | collective-permute-start | bytes 196616 | tf_op jit(solution)/shard_map/ppermute | solution.py:181
  37.8 4.6 %copy-done.1 = f32[768,4096]{1,0:T(8,128)S(1)} copy-done((f32[768,4096]{1,0:T(8,128)S(1)}, f32[768,4096]{1,0:T(8,128)}, u32[]{:S(2)}) %copy-start.1) | copy-done | bytes 12582936
  42.3 3.2 %shard_map.43 = (f32[128,1024]{1,0:T(8,128)S(1)}, f32[128,1024]{1,0:T(8,128)S(1)}) custom-call(s32[2]{0:T(128)S(1)} %get-tuple-element.35.index_ref, bf16[256,768]{1,0:T(8,128)(2,1)S(1)} %get-tuple-element.15.pair_ref, f32[768,4096]{1,0:T(8,128)S(1)} %copy-done.1), custom_call_target="tpu_custom_call" | custom-call | tf_op jit(solution)/shard_map/pallas_call | solution.py:129
  45.6 1.6 %collective-permute-start.7 = (f32[128,1024]{1,0:T(8,128)S(1)}, f32[128,1024]{1,0:T(8,128)}, u32[]{:S(2)}, u32[]{:S(2)}) collective-permute-start(f32[128,1024]{1,0:T(8,128)S(1)} %get-tuple-element.19), channel_id=1, source_target_pairs={{0,4},{2,6},{4,0},{6,2},{8,12},{10,14},{12,8},{14,10},{16,20},{18,... | collective-permute-start | bytes 1572872 | tf_op jit(solution)/shard_map/ppermute | solution.py:181
  47.2 0.0 collective-permute-done.4
  47.2 0.1 copy.6
  47.3 11.7 %cholesky.17 = f32[128,128]{1,0:T(8,128)S(1)} custom-call(f32[128,128]{1,0:T(8,128)S(1)} %fusion.3), custom_call_target="Cholesky" | custom-call | tf_op jit(solution)/shard_map/jit(cholesky)/cholesky | solution.py:213
  59.0 0.6 compare_reduce_fusion
  59.7 0.0 collective-permute-done.5
  59.7 0.1 dynamic-slice_add_fusion.2
  59.8 0.6 collective-permute-start.6
  60.3 1.1 %dynamic-slice_add_fusion = (f32[128,512]{1,0:T(8,128)S(1)}, f32[128,512]{1,0:T(8,128)S(1)}) fusion(f32[128,1024]{1,0:T(8,128)} %collective-permute-done.7, s32[]{:T(128)S(6)} %select_n.76, f32[128,1024]{1,0:T(8,128)S(1)} %get-tuple-element.18, s32[]{:T(128)S(6)} %select_n.75), kind=kLoop, calls=%fused_computation.1 | loop fusion | flops 131072 | bytes 1572872 | tf_op jit(solution)/shard_map/add | solution.py:208
  61.5 0.6 collective-permute-start.8
  62.1 0.7 fusion
  62.7 9.8 %custom-call.7 = f32[1,128,128]{1,2,0:T(8,128)S(1)} custom-call(f32[1,128,128]{2,1,0:T(8,128)S(1)} %fusion), custom_call_target="InvertDiagBlocksLowerTriangular" | custom-call | tf_op jit(solution)/shard_map/jit(_solve_triangular)/triangular_solve | solution.py:214
  72.5 0.2 fusion.1.inverse_ref
  72.8 0.0 collective-permute-done.6.b_ref
  72.8 1.0 %shard_map.45 = (f32[32,1024]{1,0:T(8,128)S(1)}, f32[32,1024]{1,0:T(8,128)S(1)}, f32[32,1024]{1,0:T(8,128)S(1)}, f32[32,1024]{1,0:T(8,128)S(1)}) custom-call(s32[1]{0:T(128)} %bitcast.3.index_ref, f32[128,128]{1,0:T(8,128)S(1)} %fusion.1.inverse_ref, f32[128,512]{1,0:T(8,128)S(1)} %get-tuple-element.27.a_ref, f32[128,512]{1,0:T(8,128)S(1)} %collective-permute-done.6.b_ref, ...), custom_call_target="tpu_custom_call" | custom-call | tf_op jit(solution)/shard_map/pallas_call | solution.py:163
  73.8 0.4 collective-permute-start.10
  74.2 2.5 %collective-permute-start.11 = (f32[32,1024]{1,0:T(8,128)S(1)}, f32[32,1024]{1,0:T(8,128)S(1)}, u32[]{:S(2)}, u32[]{:S(2)}) collective-permute-start(f32[32,1024]{1,0:T(8,128)S(1)} %get-tuple-element.23), channel_id=1, source_target_pairs={{0,24},{2,26},{4,28},{6,30},{8,16},{10,18},{12,20},{14,22},{16,8},... | collective-permute-start | bytes 393224 | tf_op jit(solution)/shard_map/ppermute | solution.py:181
  76.7 0.7 collective-permute-start.9
  77.4 6.0 %collective-permute-done.10 = f32[32,1024]{1,0:T(8,128)S(1)} collective-permute-done((f32[32,1024]{1,0:T(8,128)S(1)}, f32[32,1024]{1,0:T(8,128)S(1)}, u32[]{:S(2)}, u32[]{:S(2)}) %collective-permute-start.10) | collective-permute-done | bytes 131104 | tf_op jit(solution)/shard_map/ppermute | solution.py:181
  83.3 0.6 collective-permute-done.9
  84.0 2.5 %collective-permute-start.12 = (f32[8,1024]{1,0:T(8,128)S(1)}, f32[8,1024]{1,0:T(8,128)S(1)}, u32[]{:S(2)}, u32[]{:S(2)}) collective-permute-start(f32[8,1024]{1,0:T(8,128)S(1)} %get-tuple-element.34), channel_id=1, source_target_pairs={{0,6},{2,4},{4,2},{6,0},{8,14},{10,12},{12,10},{14,8},{16,22},{18,... | collective-permute-start | bytes 98312 | tf_op jit(solution)/shard_map/ppermute | solution.py:181
  86.5 0.5 collective-permute-start.13
  87.0 0.5 collective-permute-start.14
  87.5 1.2 %convolution_multiply_fusion = f32[768,128]{1,0:T(8,128)} fusion(f32[768,128]{1,0:T(8,128)S(1)} %get-tuple-element.13, f32[128,128]{1,0:T(8,128)S(1)} %fusion.1.inverse_ref), kind=kOutput, calls=%fused_computation | convolution fusion | flops 151093248 | bytes 851968 | tf_op jit(solution)/shard_map/dot_general | solution.py:234
  88.8 0.1 collective-permute-done.12
  88.9 1.5 %collective-permute-done.13 = f32[8,1024]{1,0:T(8,128)S(1)} collective-permute-done((f32[8,1024]{1,0:T(8,128)S(1)}, f32[8,1024]{1,0:T(8,128)S(1)}, u32[]{:S(2)}, u32[]{:S(2)}) %collective-permute-start.13) | collective-permute-done | bytes 32800 | tf_op jit(solution)/shard_map/ppermute | solution.py:181
  90.4 0.5 collective-permute-done.14
  91.0 0.0 copy-start.3
  91.1 0.6 copy-done.3
  (23 shorter events, 0.2 us)
Async XLA Ops:
  0.6 1.6 %copy-start.2 = (s32[4096,128]{1,0:T(8,128)S(1)}, s32[4096,128]{1,0:T(8,128)}, u32[]{:S(2)}) copy-start(s32[4096,128]{1,0:T(8,128)} %sign_ref.1) | copy-start | bytes 6291460
  11.4 1.9 %collective-permute-start = (f32[768,128]{1,0:T(8,128)S(1)}, f32[768,128]{1,0:T(8,128)S(1)}, u32[]{:S(2)}, u32[]{:S(2)}) collective-permute-start(f32[768,128]{1,0:T(8,128)S(1)} %shard_map.41.refs_0_), channel_id=1, source_target_pairs={{0,1},{1,0},{2,3},{3,2},{4,5},{5,4},{6,7},{7,6},{8,9},{9,8},{10,11... | collective-permute-start | bytes 1179656 | tf_op jit(solution)/shard_map/ppermute | solution.py:188
  13.9 5.3 %collective-permute-start.1 = (f32[128,128]{0,1:T(8,128)S(1)}, f32[128,128]{0,1:T(8,128)S(1)}, u32[]{:S(2)}, u32[]{:S(2)}) collective-permute-start(f32[128,128]{0,1:T(8,128)S(1)} %copy.5), channel_id=1, source_target_pairs={{0,2},{2,0},{4,6},{6,4},{8,10},{10,8},{12,14},{14,12},{16,18},{18,... | collective-permute-start | bytes 196616 | tf_op jit(solution)/shard_map/ppermute | solution.py:181
  19.3 4.3 %collective-permute-start.2 = (f32[128,128]{0,1:T(8,128)S(1)}, f32[128,128]{0,1:T(8,128)S(1)}, u32[]{:S(2)}, u32[]{:S(2)}) collective-permute-start(f32[128,128]{0,1:T(8,128)S(1)} %add.76), channel_id=1, source_target_pairs={{0,4},{2,6},{4,0},{6,2},{8,12},{10,14},{12,8},{14,10},{16,20},{18,... | collective-permute-start | bytes 196616 | tf_op jit(solution)/shard_map/ppermute | solution.py:181
  23.6 11.5 %collective-permute-start.3 = (f32[128,128]{0,1:T(8,128)S(1)}, f32[128,128]{0,1:T(8,128)S(1)}, u32[]{:S(2)}, u32[]{:S(2)}) collective-permute-start(f32[128,128]{0,1:T(8,128)S(1)} %add.77), channel_id=1, source_target_pairs={{0,8},{2,10},{4,12},{6,14},{8,0},{10,2},{12,4},{14,6},{16,24},{18,... | collective-permute-start | bytes 196616 | tf_op jit(solution)/shard_map/ppermute | solution.py:181
  25.7 4.6 %copy-start = (f32[768,4096]{1,0:T(8,128)S(1)}, f32[768,4096]{1,0:T(8,128)}, u32[]{:S(2)}) copy-start(f32[768,4096]{1,0:T(8,128)} %dev_ref.5) | copy-start | bytes 37748740
  33.5 26.2 %collective-permute-start.5 = (f32[128,1024]{1,0:T(8,128)S(1)}, f32[128,1024]{1,0:T(8,128)S(1)}, u32[]{:S(2)}, u32[]{:S(2)}) collective-permute-start(f32[128,1024]{1,0:T(8,128)S(1)} %get-tuple-element.17), channel_id=1, source_target_pairs={{0,2},{2,0},{4,6},{6,4},{8,10},{10,8},{12,14},{14,12},{16,18},{18,... | collective-permute-start | bytes 1572872 | tf_op jit(solution)/shard_map/ppermute | solution.py:181
  35.1 12.1 %collective-permute-start.4 = (f32[128,128]{0,1:T(8,128)S(1)}, f32[128,128]{0,1:T(8,128)S(1)}, u32[]{:S(2)}, u32[]{:S(2)}) collective-permute-start(f32[128,128]{0,1:T(8,128)S(1)} %add.78), channel_id=1, source_target_pairs={{0,16},{2,18},{4,20},{6,22},{8,24},{10,26},{12,28},{14,30},{16,0},... | collective-permute-start | bytes 196616 | tf_op jit(solution)/shard_map/ppermute | solution.py:181
  37.8 4.6 %copy-start.1 = (f32[768,4096]{1,0:T(8,128)S(1)}, f32[768,4096]{1,0:T(8,128)}, u32[]{:S(2)}) copy-start(f32[768,4096]{1,0:T(8,128)} %dev_ref.5) | copy-start | bytes 37748740
  45.6 14.8 %collective-permute-start.7 = (f32[128,1024]{1,0:T(8,128)S(1)}, f32[128,1024]{1,0:T(8,128)}, u32[]{:S(2)}, u32[]{:S(2)}) collective-permute-start(f32[128,1024]{1,0:T(8,128)S(1)} %get-tuple-element.19), channel_id=1, source_target_pairs={{0,4},{2,6},{4,0},{6,2},{8,12},{10,14},{12,8},{14,10},{16,20},{18,... | collective-permute-start | bytes 1572872 | tf_op jit(solution)/shard_map/ppermute | solution.py:181
  59.8 13.0 %collective-permute-start.6 = (f32[128,512]{1,0:T(8,128)S(1)}, f32[128,512]{1,0:T(8,128)S(1)}, u32[]{:S(2)}, u32[]{:S(2)}) collective-permute-start(f32[128,512]{1,0:T(8,128)S(1)} %get-tuple-element.26), channel_id=1, source_target_pairs={{0,4},{2,6},{4,0},{6,2},{8,12},{10,14},{12,8},{14,10},{16,20},{18,... | collective-permute-start | bytes 786440 | tf_op jit(solution)/shard_map/ppermute | solution.py:181
  61.5 11.3 %collective-permute-start.8 = (f32[128,512]{1,0:T(8,128)S(1)}, f32[128,512]{1,0:T(8,128)S(1)}, u32[]{:S(2)}, u32[]{:S(2)}) collective-permute-start(f32[128,512]{1,0:T(8,128)S(1)} %get-tuple-element.24), channel_id=1, source_target_pairs={{0,2},{2,0},{4,6},{6,4},{8,10},{10,8},{12,14},{14,12},{16,18},{18,... | collective-permute-start | bytes 786440 | tf_op jit(solution)/shard_map/ppermute | solution.py:181
  73.8 9.5 %collective-permute-start.10 = (f32[32,1024]{1,0:T(8,128)S(1)}, f32[32,1024]{1,0:T(8,128)S(1)}, u32[]{:S(2)}, u32[]{:S(2)}) collective-permute-start(f32[32,1024]{1,0:T(8,128)S(1)} %get-tuple-element.22), channel_id=1, source_target_pairs={{0,16},{2,18},{4,20},{6,22},{8,24},{10,26},{12,28},{14,30},{16,0},... | collective-permute-start | bytes 393224 | tf_op jit(solution)/shard_map/ppermute | solution.py:181
  74.2 9.1 %collective-permute-start.11 = (f32[32,1024]{1,0:T(8,128)S(1)}, f32[32,1024]{1,0:T(8,128)S(1)}, u32[]{:S(2)}, u32[]{:S(2)}) collective-permute-start(f32[32,1024]{1,0:T(8,128)S(1)} %get-tuple-element.23), channel_id=1, source_target_pairs={{0,24},{2,26},{4,28},{6,30},{8,16},{10,18},{12,20},{14,22},{16,8},... | collective-permute-start | bytes 393224 | tf_op jit(solution)/shard_map/ppermute | solution.py:181
  76.7 7.3 %collective-permute-start.9 = (f32[32,1024]{1,0:T(8,128)S(1)}, f32[32,1024]{1,0:T(8,128)S(1)}, u32[]{:S(2)}, u32[]{:S(2)}) collective-permute-start(f32[32,1024]{1,0:T(8,128)S(1)} %get-tuple-element.21), channel_id=1, source_target_pairs={{0,8},{2,10},{4,12},{6,14},{8,0},{10,2},{12,4},{14,6},{16,24},{18,... | collective-permute-start | bytes 393224 | tf_op jit(solution)/shard_map/ppermute | solution.py:181
  84.0 4.9 %collective-permute-start.12 = (f32[8,1024]{1,0:T(8,128)S(1)}, f32[8,1024]{1,0:T(8,128)S(1)}, u32[]{:S(2)}, u32[]{:S(2)}) collective-permute-start(f32[8,1024]{1,0:T(8,128)S(1)} %get-tuple-element.34), channel_id=1, source_target_pairs={{0,6},{2,4},{4,2},{6,0},{8,14},{10,12},{12,10},{14,8},{16,22},{18,... | collective-permute-start | bytes 98312 | tf_op jit(solution)/shard_map/ppermute | solution.py:181
  86.5 3.9 %collective-permute-start.13 = (f32[8,1024]{1,0:T(8,128)S(1)}, f32[8,1024]{1,0:T(8,128)S(1)}, u32[]{:S(2)}, u32[]{:S(2)}) collective-permute-start(f32[8,1024]{1,0:T(8,128)S(1)} %get-tuple-element.33), channel_id=1, source_target_pairs={{0,4},{2,6},{4,0},{6,2},{8,12},{10,14},{12,8},{14,10},{16,20},{18,... | collective-permute-start | bytes 98312 | tf_op jit(solution)/shard_map/ppermute | solution.py:181
  87.0 3.9 %collective-permute-start.14 = (f32[8,1024]{1,0:T(8,128)S(1)}, f32[8,1024]{1,0:T(8,128)S(1)}, u32[]{:S(2)}, u32[]{:S(2)}) collective-permute-start(f32[8,1024]{1,0:T(8,128)S(1)} %get-tuple-element.32), channel_id=1, source_target_pairs={{0,2},{2,0},{4,6},{6,4},{8,10},{10,8},{12,14},{14,12},{16,18},{18,... | collective-permute-start | bytes 98312 | tf_op jit(solution)/shard_map/ppermute | solution.py:181
  91.0 0.7 copy-start.3

commit v2 on v0

v2 whole, which is shorter than its diff:
```python
import functools
import math

import jax
import jax.numpy as jnp
from jax import lax
from jax.experimental import pallas as pl
from jax.experimental.pallas import tpu as pltpu
from jax.sharding import PartitionSpec as P

SCANS = 8192

precise = lax.Precision.HIGHEST
MIB = 1 << 20


def split(value):
    high = value.astype(jnp.bfloat16)
    low = (value - high.astype(jnp.float32)).astype(jnp.bfloat16)
    return high, low


def dot(a, b):
    return jnp.dot(a, b, preferred_element_type=jnp.float32)


def vmem():
    return pl.BlockSpec(memory_space=pltpu.VMEM)


def place():
    me = lax.axis_index("rows")
    return me & 1, (me >> 1) & 1, me


def params(mib):
    return pltpu.CompilerParams(vmem_limit_bytes=mib * MIB)


def sketch_kernel(unit, gain, depth, dev_hbm, sign_hbm, high_ref, low_ref, out_ref, dev_buf, sign_buf, omega, dev_sem, sign_sem):
    block = dev_buf.shape[1]
    steps = high_ref.shape[0] // block
    signs = pltpu.make_async_copy(sign_hbm, sign_buf, sign_sem)
    signs.start()

    def fetch(i):
        return pltpu.make_async_copy(
            dev_hbm.at[pl.ds(i * block, block), :], dev_buf.at[i % depth], dev_sem.at[i % depth]
        )

    for i in range(min(depth - 1, steps)):
        fetch(i).start()
    signs.wait()
    omega[...] = (sign_buf[...].astype(jnp.float32) * unit).astype(jnp.bfloat16)
    for i in range(steps):
        if i + depth - 1 < steps:
            fetch(i + depth - 1).start()
        fetch(i).wait()
        here = slice(i * block, (i + 1) * block)
        high, low = split(dev_buf[i % depth])
        high_ref[here, :] = high
        low_ref[here, :] = low
        out_ref[here, :] = (dot(high, omega[...]) + dot(low, omega[...])) * gain


def sketch_of(dev, signs):
    rows, cols = dev.shape
    rank = signs.shape[1]
    block, depth = rows // 4, 3
    unit = 2.0 ** -math.ceil(math.log2(math.sqrt(SCANS)))
    gain = 1.0 / (math.sqrt(SCANS) * unit)
    dev = pltpu.with_memory_space_constraint(dev, pltpu.HBM)
    signs = pltpu.with_memory_space_constraint(signs, pltpu.HBM)
    return pl.pallas_call(
        functools.partial(sketch_kernel, unit, gain, depth),
        in_specs=[pl.BlockSpec(memory_space=pltpu.HBM)] * 2,
        out_specs=[vmem()] * 3,
        out_shape=[pltpu.VMEM((rows, cols), jnp.bfloat16)] * 2 + [pltpu.VMEM((rows, rank), jnp.float32)],
        scratch_shapes=[
            pltpu.VMEM((depth, block, cols), jnp.float32),
            pltpu.VMEM((cols, rank), jnp.int32),
            pltpu.VMEM((cols, rank), jnp.bfloat16),
            pltpu.SemaphoreType.DMA((depth,)),
            pltpu.SemaphoreType.DMA,
        ],
        compiler_params=params(24),
        name="sketch",
    )(dev, signs)


def gram_kernel(parts, *refs):
    total_ref, pair_ref, gram_ref = refs[parts:]
    total = refs[0][...]
    for ref in refs[1:parts]:
        total = total + ref[...]
    total_ref[...] = total
    flat = total.T
    high, low = split(flat)
    rank = flat.shape[0]
    pair_ref[:rank, :] = high
    pair_ref[rank:, :] = low
    gram_ref[...] = lax.dot_general(
        flat, total, (((1,), (0,)), ((), ())),
        precision=precise, preferred_element_type=jnp.float32,
    )


def gram_of(*sketches):
    rows, rank = sketches[0].shape
    return pl.pallas_call(
        functools.partial(gram_kernel, len(sketches)),
        in_specs=[vmem()] * len(sketches),
        out_specs=[vmem()] * 3,
        out_shape=[
            jax.ShapeDtypeStruct((rows, rank), jnp.float32),
            jax.ShapeDtypeStruct((2 * rank, rows), jnp.bfloat16),
            jax.ShapeDtypeStruct((rank, rank), jnp.float32),
        ],
        compiler_params=params(8),
        name="gram",
    )(*sketches)


def cross_kernel(block, stay, pair_ref, high_ref, low_ref, *outs):
    rank, width = outs[0].shape
    x, y = place()[:2]
    chunks = (x, 2 + y) if stay else (1 - x, 3 - y)
    for chunk, out in zip(chunks, outs):
        for t in range(width // block):
            start = pl.multiple_of(chunk * width + t * block, 128)
            high = high_ref[:, pl.ds(start, block)]
            low = low_ref[:, pl.ds(start, block)]
            both = dot(pair_ref[...], high)
            out[:, t * block:(t + 1) * block] = (both[:rank] + both[rank:]) + dot(pair_ref[:rank, :], low)


def cross_of(stay, pair, high, low):
    rank, rows = pair.shape[0] // 2, pair.shape[1]
    width = high.shape[1] // 4
    return pl.pallas_call(
        functools.partial(cross_kernel, min(512, width), stay),
        in_specs=[vmem()] * 3,
        out_specs=[vmem()] * 2,
        out_shape=[jax.ShapeDtypeStruct((rank, width), jnp.float32)] * 2,
        compiler_params=params(8),
        cost_estimate=pl.CostEstimate(flops=12 * rank * rows * width, bytes_accessed=8 * rows * width, transcendentals=0),
        name="cross_stay" if stay else "cross_leave",
    )(pair, high, low)


def thirds(value):
    high = value.astype(jnp.bfloat16)
    rest = value - high.astype(jnp.float32)
    middle = rest.astype(jnp.bfloat16)
    low = (rest - middle.astype(jnp.float32)).astype(jnp.bfloat16)
    return high, middle, low


def inverse_kernel(gram_ref, out_ref, work):
    rank = gram_ref.shape[0]
    rows = lax.broadcasted_iota(jnp.int32, (rank, rank), 0)
    lanes = lax.broadcasted_iota(jnp.int32, (rank, rank), 1)
    work[:, :rank] = gram_ref[...]
    work[:, rank:] = jnp.where(rows == lanes, 1.0, 0.0)
    for base in range(0, rank, 8):
        left = work[base:base + 8, :rank]
        block = {}
        for j in range(8):
            column = jnp.broadcast_to(left[:, base + j:base + j + 1], (8, rank))
            for i in range(j, 8):
                block[i, j] = column[i:i + 1, :]
        a = [work[base + i:base + i + 1, :rank] for i in range(8)]
        e = [work[base + i:base + i + 1, rank:] for i in range(8)]
        for j in range(8):
            scale = lax.rsqrt(block[j, j])
            a[j] = a[j] * scale
            e[j] = e[j] * scale
            factor = {i: block[i, j] * scale for i in range(j + 1, 8)}
            for i in range(j + 1, 8):
                for k in range(j + 1, i + 1):
                    block[i, k] = block[i, k] - factor[i] * factor[k]
                a[i] = a[i] - factor[i] * a[j]
                e[i] = e[i] - factor[i] * e[j]
            work[base + j:base + j + 1, :rank] = a[j]
            work[base + j:base + j + 1, rank:] = e[j]
        if base + 8 < rank:
            high, middle, low = thirds(work[base:base + 8, :])
            first = jnp.concatenate([high, high, middle, middle, high, low], axis=0)[:, :rank]
            second = jnp.concatenate([high, middle, high, middle, low, high], axis=0)
            update = lax.dot_general(
                first, second, (((0,), (0,)), ((), ())), preferred_element_type=jnp.float32
            )
            work[base + 8:, :] = work[base + 8:, :] - update[base + 8:, :]
    out_ref[...] = jnp.where(lanes <= rows, work[:, rank:], 0.0)


def inverse_of(gram):
    rank = gram.shape[0]
    return pl.pallas_call(
        inverse_kernel,
        in_specs=[vmem()],
        out_specs=vmem(),
        out_shape=jax.ShapeDtypeStruct((rank, rank), jnp.float32),
        scratch_shapes=[pltpu.VMEM((rank, 2 * rank), jnp.float32)],
        compiler_params=params(8),
        cost_estimate=pl.CostEstimate(flops=8 * 10**9, bytes_accessed=10**6, transcendentals=0),
        name="inverse",
    )(gram)


def onward_kernel(axis, keep_ref, got_ref, out_ref):
    half = out_ref.shape[1]
    here = pl.ds(pl.multiple_of((1 - place()[axis]) * half, 128), half)
    out_ref[...] = keep_ref[:, here] + got_ref[:, here]


def onward(axis, keep, got):
    rank, width = keep.shape
    return pl.pallas_call(
        functools.partial(onward_kernel, axis),
        in_specs=[vmem()] * 2,
        out_specs=vmem(),
        out_shape=jax.ShapeDtypeStruct((rank, width // 2), jnp.float32),
        compiler_params=params(8),
        name="onward",
    )(keep, got)


def project_kernel(n, inverse_ref, keep_x, got_x, then_x, keep_y, got_y, then_y, *refs):
    outs, ordered = refs[:-1], refs[-1]
    group, half = outs[0].shape[0], then_x.shape[1]
    each = ordered.shape[0] // n
    x, y, me = place()
    for i in range(n):
        ordered[i * each:(i + 1) * each, :] = inverse_ref[pl.ds((me ^ i) * each, each), :]
    at_x = pl.ds(pl.multiple_of(y * half, 128), half)
    at_y = pl.ds(pl.multiple_of(x * half, 128), half)
    left = (keep_x[:, at_x] + got_x[:, at_x]) + then_x[...]
    right = (keep_y[:, at_y] + got_y[:, at_y]) + then_y[...]
    left = jnp.dot(ordered[...], left, precision=precise, preferred_element_type=jnp.float32)
    right = jnp.dot(ordered[...], right, precision=precise, preferred_element_type=jnp.float32)
    for k, out in enumerate(outs):
        out[:, :half] = left[k * group:(k + 1) * group]
        out[:, half:] = right[k * group:(k + 1) * group]


def project(n, inverse, *parts):
    rank, half = parts[2].shape
    groups = n // 4
    shape = jax.ShapeDtypeStruct((rank // groups, 2 * half), jnp.float32)
    return pl.pallas_call(
        functools.partial(project_kernel, n),
        in_specs=[vmem()] * 7,
        out_specs=[vmem()] * groups,
        out_shape=[shape] * groups,
        scratch_shapes=[pltpu.VMEM((rank, rank), jnp.float32)],
        compiler_params=params(8),
        name="project",
    )(inverse, *parts)


def collect_kernel(parts, *refs):
    outs = refs[parts:]
    each = outs[0].shape[0]
    for k, out in enumerate(outs):
        total = refs[0][k * each:(k + 1) * each, :]
        for ref in refs[1:parts]:
            total = total + ref[k * each:(k + 1) * each, :]
        out[...] = total


def collect(*parts):
    group, width = parts[0].shape
    return pl.pallas_call(
        functools.partial(collect_kernel, len(parts)),
        in_specs=[vmem()] * len(parts),
        out_specs=[vmem()] * 4,
        out_shape=[jax.ShapeDtypeStruct((group // 4, width), jnp.float32)] * 4,
        compiler_params=params(8),
        name="collect",
    )(*parts)


def assemble_kernel(*refs):
    out = refs[-1]
    half = out.shape[1] // 8
    x, y = place()[:2]
    for k, ref in enumerate(refs[:-1]):
        qx, qy = x ^ (k & 1), y ^ (k >> 1)
        out[:, pl.ds(pl.multiple_of((2 * qx + qy) * half, 128), half)] = ref[:, :half]
        out[:, pl.ds(pl.multiple_of((4 + 2 * qy + qx) * half, 128), half)] = ref[:, half:]


def assemble(*blocks):
    each, width = blocks[0].shape
    return pl.pallas_call(
        assemble_kernel,
        in_specs=[vmem()] * 4,
        out_specs=vmem(),
        out_shape=jax.ShapeDtypeStruct((each, 4 * width), jnp.float32),
        compiler_params=params(8),
        name="assemble",
    )(*blocks)


def local(deviations, test_signs):
    rows, cols = deviations.shape
    n, n_cols = lax.axis_size("rows"), lax.axis_size("cols")
    samples = rows * n

    def swap(value, bit):
        return lax.ppermute(value, "rows", [(i, i ^ bit) for i in range(n)])

    high, low, part = sketch_of(deviations, test_signs)
    step = 1
    while 2 * step < n_cols:
        part = part + lax.ppermute(part, "cols", [(i, i ^ step) for i in range(n_cols)])
        step *= 2
    other = lax.ppermute(part, "cols", [(i, i ^ step) for i in range(n_cols)])
    sketch, pair, gram = gram_of(part, other)

    leave = cross_of(False, pair, high, low)
    stay = cross_of(True, pair, high, low)

    step, beside = 1, [leave, stay]
    while step < n:
        found = [swap(gram, step * k) for k in range(1, min(4, n // step))]
        if beside:
            found, _ = lax.optimization_barrier((found, beside.pop(0)))
        for value in found:
            gram = gram + value
        step *= 4
    inverse = inverse_of(gram)

    got_x, got_y = swap(leave[0], 1), swap(leave[1], 2)
    then_x = swap(onward(1, stay[0], got_x), 2)
    then_y = swap(onward(0, stay[1], got_y), 1)

    groups = project(n, inverse, stay[0], got_x, then_x, stay[1], got_y, then_y)
    basis = lax.dot_general(
        sketch, inverse, (((1,), (1,)), ((), ())),
        precision=precise, preferred_element_type=jnp.float32,
    ) * math.sqrt(samples)
    found = [swap(groups[k], 4 * k) for k in range(1, n // 4)]
    found, basis = lax.optimization_barrier((found, basis))

    blocks = collect(groups[0], *found)
    blocks = [blocks[0]] + [swap(blocks[k], k) for k in range(1, 4)]
    return (basis, assemble(*blocks))


def solution(mesh):
    return jax.shard_map(
        local,
        mesh=mesh,
        in_specs=(P("rows", "cols"), P("cols", None)),
        out_specs=(P("rows", None), P("rows", "cols")),
        check_vma=False,
    )
```

time: 279 us -> 58.9 us (0.21)
  waiting for transfers between devices: 208 us -> 15.8 us
  matrix products: 30.8 us -> 1.23 us
  other arithmetic: 23.7 us -> 0.03 us
  starting transfers between devices: 0.3 us -> 23.8 us
  Pallas kernels: 0 us -> 17.2 us
  between operations: 13.8 us -> 0.72 us
    psum x2 -> x0, waiting for transfers between devices: 129 us -> none  [the longest x1 108 us: rows_first(): return lax.psum(gram_part, 'rows')]
    reduce_scatter x1 -> x0, waiting for transfers between devices: 78.8 us -> none  [local(): lax.psum_scatter(lax.dot_general(orthonormal, deviations, (((0,), (0,)),...]
    dot_general x3 -> x1, matrix products: 29.3 us -> 1.23 us  [local(): lax.dot_general(sketch, inverse, (((1,), (1,)), ((), ())), precision=prec...]
    ppermute x0 -> x17, starting transfers between devices: none -> 23.8 us  [the longest x16 23.2 us: swap(): return lax.ppermute(value, 'rows', [(i, i ^ bit) for i in range(n)])]
    another operation x5 -> x0, other arithmetic: 22.9 us -> none  [the longest x3 12.4 us: orthogonalize(): tri_low = jnp.linalg.cholesky(gram_sum)]
    pallas_call x0 -> x10, Pallas kernels: none -> 17.2 us  [the longest x1 7.09 us: sketch_of(): pl.pallas_call(functools.partial(sketch_kernel, unit, gain, depth), in_sp...]
    ppermute x0 -> x17, waiting for transfers between devices: none -> 15.8 us  [the longest x16 14.4 us: swap(): return lax.ppermute(value, 'rows', [(i, i ^ bit) for i in range(n)])]
  transfers between devices with their start and end apart: 3 -> 17, of which waited for: 3 -> 9; matrix products, arithmetic and copies ran while one was open for 0% -> 2% of each run, Pallas kernels for 0% -> 14%
where the time goes in v2:
time: 58.9 us; the launch traced here: 58.8 us
  starting transfers between devices  23.8 us (40%)
  Pallas kernels  17.2 us (29%)
  waiting for transfers between devices  15.8 us (27%)
  matrix products  1.23 us (2%)
  between operations  0.72 us (1%)
    ppermute x16, starting transfers between devices, swap(): return lax.ppermute(value, 'rows', [(i, i ^ bit) for i in range(n)])  23.2 us
    ppermute x16, waiting for transfers between devices, swap(): return lax.ppermute(value, 'rows', [(i, i ^ bit) for i in range(n)])  14.4 us
    pallas_call x1, Pallas kernels, sketch_of(): pl.pallas_call(functools.partial(sketch_kernel, unit, gain, depth), in_sp...  7.09 us
    pallas_call x1, Pallas kernels, inverse_of(): pl.pallas_call(inverse_kernel, in_specs=[vmem()], out_specs=vmem(), out_s...  5.39 us
    pallas_call x2, Pallas kernels, cross_of(): pl.pallas_call(functools.partial(cross_kernel, min(512, width), stay), in...  2.83 us
    ppermute x1, waiting for transfers between devices, local(): other = lax.ppermute(part, 'cols', [(i, i ^ step) for i in range(n_cols)])  1.35 us
    dot_general x1, matrix products, local(): lax.dot_general(sketch, inverse, (((1,), (1,)), ((), ())), precision=prec...  1.23 us
  transfers between devices with their start and end apart: 17, of which 9 were waited for; matrix products, arithmetic and copies ran while one was open for 2% of the time, Pallas kernels for 14%

profile of v2, /device:TPU:0, one launch (start us, length us, event | category | flops | bytes accessed | tf_op | source)
XLA Modules:
  0.0 58.8 jit_solution(15395299606907208717)
XLA Ops:
  0.6 7.1 %sketch.1 = (bf16[768,4096]{1,0:T(8,128)(2,1)S(1)}, bf16[768,4096]{1,0:T(8,128)(2,1)S(1)}, f32[768,128]{1,0:T(8,128)S(1)}) custom-call(f32[768,4096]{1,0:T(8,128)} %dev_hbm.1, s32[4096,128]{1,0:T(8,128)} %sign_hbm.1), custom_call_target="tpu_custom_call" | custom-call | tf_op jit(solution)/shard_map/sketch/pallas_call | solution.py:74
  7.7 0.5 collective-permute-start
  8.2 1.3 %collective-permute-done.refs_1_ = f32[768,128]{1,0:T(8,128)S(1)} collective-permute-done((f32[768,128]{1,0:T(8,128)S(1)}, f32[768,128]{1,0:T(8,128)S(1)}, u32[]{:S(2)}, u32[]{:S(2)}) %collective-permute-start) | collective-permute-done | bytes 393248 | tf_op jit(solution)/shard_map/ppermute | solution.py:319
  9.6 0.5 gram.1
  10.2 3.9 %collective-permute-start.3 = (f32[128,128]{1,0:T(8,128)S(1)}, f32[128,128]{1,0:T(8,128)S(1)}, u32[]{:S(2)}, u32[]{:S(2)}) collective-permute-start(f32[128,128]{1,0:T(8,128)S(1)} %get-tuple-element.31), channel_id=1, source_target_pairs={{0,6},{2,4},{4,2},{6,0},{8,14},{10,12},{12,10},{14,8},{16,22},{18,... | collective-permute-start | bytes 196616 | tf_op jit(solution)/shard_map/ppermute | solution.py:312
  14.0 0.5 collective-permute-start.2
  14.5 0.1 collective-permute-start.1
  14.7 1.4 %cross_leave.1 = (f32[128,1024]{1,0:T(8,128)S(1)}, f32[128,1024]{1,0:T(8,128)S(1)}) custom-call(bf16[256,768]{1,0:T(8,128)(2,1)S(1)} %get-tuple-element.32.pair_ref, bf16[768,4096]{1,0:T(8,128)(2,1)S(1)} %get-tuple-element.33.high_ref, bf16[768,4096]{1,0:T(8,128)(2,1)S(1)} %get-tuple-element.34.low_ref), custom_call_target="tpu_custom_call" | custom-call | flops 1207959552 | bytes 6291456 | tf_op jit(solution)/shard_map/cross_leave/pallas_call | solution.py:140
  16.1 2.0 %collective-permute-start.7 = (f32[128,1024]{1,0:T(8,128)S(1)}, f32[128,1024]{1,0:T(8,128)S(1)}, u32[]{:S(2)}, u32[]{:S(2)}) collective-permute-start(f32[128,1024]{1,0:T(8,128)S(1)} %get-tuple-element.35), channel_id=1, source_target_pairs={{0,2},{2,0},{4,6},{6,4},{8,10},{10,8},{12,14},{14,12},{16,18},{18,... | collective-permute-start | bytes 1572872 | tf_op jit(solution)/shard_map/ppermute | solution.py:312
  18.1 1.5 %collective-permute-start.9 = (f32[128,1024]{1,0:T(8,128)S(1)}, f32[128,1024]{1,0:T(8,128)S(1)}, u32[]{:S(2)}, u32[]{:S(2)}) collective-permute-start(f32[128,1024]{1,0:T(8,128)S(1)} %get-tuple-element.36), channel_id=1, source_target_pairs={{0,4},{2,6},{4,0},{6,2},{8,12},{10,14},{12,8},{14,10},{16,20},{18,... | collective-permute-start | bytes 1572872 | tf_op jit(solution)/shard_map/ppermute | solution.py:312
  19.6 0.0 collective-permute-done.3
  19.6 0.0 collective-permute-done.2
  19.6 0.0 collective-permute-done.1
  19.6 3.7 %collective-permute-start.6 = (f32[128,128]{1,0:T(8,128)S(1)}, f32[128,128]{1,0:T(8,128)S(1)}, u32[]{:S(2)}, u32[]{:S(2)}) collective-permute-start(f32[128,128]{1,0:T(8,128)S(1)} %add_add_fusion.1), channel_id=1, source_target_pairs={{0,24},{2,26},{4,28},{6,30},{8,16},{10,18},{12,20},{14,22},{16,8},... | collective-permute-start | bytes 196616 | tf_op jit(solution)/shard_map/ppermute | solution.py:312
  23.3 0.0 collective-permute-start.5
  23.3 0.8 %collective-permute-start.4 = (f32[128,128]{1,0:T(8,128)S(1)}, f32[128,128]{1,0:T(8,128)S(1)}, u32[]{:S(2)}, u32[]{:S(2)}) collective-permute-start(f32[128,128]{1,0:T(8,128)S(1)} %add_add_fusion.1), channel_id=1, source_target_pairs={{0,8},{2,10},{4,12},{6,14},{8,0},{10,2},{12,4},{14,6},{16,24},{18,... | collective-permute-start | bytes 196616 | tf_op jit(solution)/shard_map/ppermute | solution.py:312
  24.1 1.4 %cross_stay.1 = (f32[128,1024]{1,0:T(8,128)S(1)}, f32[128,1024]{1,0:T(8,128)S(1)}) custom-call(bf16[256,768]{1,0:T(8,128)(2,1)S(1)} %get-tuple-element.32.pair_ref, bf16[768,4096]{1,0:T(8,128)(2,1)S(1)} %get-tuple-element.33.high_ref, bf16[768,4096]{1,0:T(8,128)(2,1)S(1)} %get-tuple-element.34.low_ref), custom_call_target="tpu_custom_call" | custom-call | flops 1207959552 | bytes 6291456 | tf_op jit(solution)/shard_map/cross_stay/pallas_call | solution.py:140
  25.5 0.3 collective-permute-done.6
  25.8 2.8 %collective-permute-done.5 = f32[128,128]{1,0:T(8,128)S(1)} collective-permute-done((f32[128,128]{1,0:T(8,128)S(1)}, f32[128,128]{1,0:T(8,128)S(1)}, u32[]{:S(2)}, u32[]{:S(2)}) %collective-permute-start.5) | collective-permute-done | bytes 65568 | tf_op jit(solution)/shard_map/ppermute | solution.py:312
  28.5 0.0 collective-permute-done.4
  28.5 1.5 %collective-permute-done.7.got_ref.got_x = f32[128,1024]{1,0:T(8,128)S(1)} collective-permute-done((f32[128,1024]{1,0:T(8,128)S(1)}, f32[128,1024]{1,0:T(8,128)S(1)}, u32[]{:S(2)}, u32[]{:S(2)}) %collective-permute-start.7) | collective-permute-done | bytes 524320 | tf_op jit(solution)/shard_map/ppermute | solution.py:312
  30.1 1.6 %collective-permute-start.8 = (f32[128,512]{1,0:T(8,128)S(1)}, f32[128,512]{1,0:T(8,128)S(1)}, u32[]{:S(2)}, u32[]{:S(2)}) collective-permute-start(f32[128,512]{1,0:T(8,128)S(1)} %onward.2), channel_id=1, source_target_pairs={{0,4},{2,6},{4,0},{6,2},{8,12},{10,14},{12,8},{14,10},{16,20},{18,... | collective-permute-start | bytes 786440 | tf_op jit(solution)/shard_map/ppermute | solution.py:312
  31.7 0.0 collective-permute-done.9.got_ref.got_y
  31.7 1.2 %collective-permute-start.10 = (f32[128,512]{1,0:T(8,128)S(1)}, f32[128,512]{1,0:T(8,128)S(1)}, u32[]{:S(2)}, u32[]{:S(2)}) collective-permute-start(f32[128,512]{1,0:T(8,128)S(1)} %onward.3), channel_id=1, source_target_pairs={{0,2},{2,0},{4,6},{6,4},{8,10},{10,8},{12,14},{14,12},{16,18},{18,... | collective-permute-start | bytes 786440 | tf_op jit(solution)/shard_map/ppermute | solution.py:312
  32.9 5.4 %inverse.1.inverse_ref = f32[128,128]{1,0:T(8,128)S(1)} custom-call(f32[128,128]{1,0:T(8,128)S(1)} %add_add_fusion.gram_ref), custom_call_target="tpu_custom_call" | custom-call | flops 8000000000 | bytes 1000000 | tf_op jit(solution)/shard_map/inverse/pallas_call | solution.py:199
  38.3 0.0 collective-permute-done.8.then_x
  38.3 0.1 collective-permute-done.10.then_y
  38.4 0.6 %project.1 = (f32[32,1024]{1,0:T(8,128)S(1)}, f32[32,1024]{1,0:T(8,128)S(1)}, f32[32,1024]{1,0:T(8,128)S(1)}, f32[32,1024]{1,0:T(8,128)S(1)}) custom-call(f32[128,128]{1,0:T(8,128)S(1)} %inverse.1.inverse_ref, f32[128,1024]{1,0:T(8,128)S(1)} %get-tuple-element.40.keep_ref.keep_x, f32[128,1024]{1,0:T(8,128)S(1)} %collective-permute-done.7.got_ref.got_x, ...), custom_call_target="tpu_custom_call" | custom-call | tf_op jit(solution)/shard_map/project/pallas_call | solution.py:251
  39.0 1.6 %collective-permute-start.11 = (f32[32,1024]{1,0:T(8,128)S(1)}, f32[32,1024]{1,0:T(8,128)S(1)}, u32[]{:S(2)}, u32[]{:S(2)}) collective-permute-start(f32[32,1024]{1,0:T(8,128)S(1)} %get-tuple-element.45), channel_id=1, source_target_pairs={{0,8},{2,10},{4,12},{6,14},{8,0},{10,2},{12,4},{14,6},{16,24},{18,... | collective-permute-start | bytes 393224 | tf_op jit(solution)/shard_map/ppermute | solution.py:312
  40.7 2.6 %collective-permute-start.12 = (f32[32,1024]{1,0:T(8,128)S(1)}, f32[32,1024]{1,0:T(8,128)S(1)}, u32[]{:S(2)}, u32[]{:S(2)}) collective-permute-start(f32[32,1024]{1,0:T(8,128)S(1)} %get-tuple-element.46), channel_id=1, source_target_pairs={{0,16},{2,18},{4,20},{6,22},{8,24},{10,26},{12,28},{14,30},{16,0},... | collective-permute-start | bytes 393224 | tf_op jit(solution)/shard_map/ppermute | solution.py:312
  43.2 0.2 collective-permute-start.13
  43.5 1.2 %convolution_multiply_fusion = f32[768,128]{1,0:T(8,128)} fusion(f32[768,128]{1,0:T(8,128)S(1)} %get-tuple-element.48, f32[128,128]{1,0:T(8,128)S(1)} %inverse.1.inverse_ref), kind=kOutput, calls=%fused_computation | convolution fusion | flops 151093248 | bytes 851968 | tf_op jit(solution)/shard_map/dot_general | solution.py:340
  44.7 0.0 collective-permute-done.11.refs_1_
  44.7 6.7 %collective-permute-done.12.refs_2_ = f32[32,1024]{1,0:T(8,128)S(1)} collective-permute-done((f32[32,1024]{1,0:T(8,128)S(1)}, f32[32,1024]{1,0:T(8,128)S(1)}, u32[]{:S(2)}, u32[]{:S(2)}) %collective-permute-start.12) | collective-permute-done | bytes 131104 | tf_op jit(solution)/shard_map/ppermute | solution.py:312
  51.4 0.0 collective-permute-done.13.refs_3_
  51.5 1.3 %collective-permute-start.14 = (f32[8,1024]{1,0:T(8,128)S(1)}, f32[8,1024]{1,0:T(8,128)S(1)}, u32[]{:S(2)}, u32[]{:S(2)}) collective-permute-start(f32[8,1024]{1,0:T(8,128)S(1)} %get-tuple-element.55), channel_id=1, source_target_pairs={{0,2},{2,0},{4,6},{6,4},{8,10},{10,8},{12,14},{14,12},{16,18},{18,... | collective-permute-start | bytes 98312 | tf_op jit(solution)/shard_map/ppermute | solution.py:312
  52.8 0.5 collective-permute-start.15
  53.3 1.8 %collective-permute-start.16 = (f32[8,1024]{1,0:T(8,128)S(1)}, f32[8,1024]{1,0:T(8,128)S(1)}, u32[]{:S(2)}, u32[]{:S(2)}) collective-permute-start(f32[8,1024]{1,0:T(8,128)S(1)} %get-tuple-element.57), channel_id=1, source_target_pairs={{0,6},{2,4},{4,2},{6,0},{8,14},{10,12},{12,10},{14,8},{16,22},{18,... | collective-permute-start | bytes 98312 | tf_op jit(solution)/shard_map/ppermute | solution.py:312
  55.0 0.4 collective-permute-done.14.refs_1_
  55.4 1.2 %collective-permute-done.15.refs_2_ = f32[8,1024]{1,0:T(8,128)S(1)} collective-permute-done((f32[8,1024]{1,0:T(8,128)S(1)}, f32[8,1024]{1,0:T(8,128)S(1)}, u32[]{:S(2)}, u32[]{:S(2)}) %collective-permute-start.15) | collective-permute-done | bytes 32800 | tf_op jit(solution)/shard_map/ppermute | solution.py:312
  56.7 1.4 %collective-permute-done.16.refs_3_ = f32[8,1024]{1,0:T(8,128)S(1)} collective-permute-done((f32[8,1024]{1,0:T(8,128)S(1)}, f32[8,1024]{1,0:T(8,128)S(1)}, u32[]{:S(2)}, u32[]{:S(2)}) %collective-permute-start.16) | collective-permute-done | bytes 32800 | tf_op jit(solution)/shard_map/ppermute | solution.py:312
  58.1 0.7 %assemble.1 = f32[8,4096]{1,0:T(8,128)} custom-call(f32[8,1024]{1,0:T(8,128)S(1)} %get-tuple-element.54.refs_0_, f32[8,1024]{1,0:T(8,128)S(1)} %collective-permute-done.14.refs_1_, f32[8,1024]{1,0:T(8,128)S(1)} %collective-permute-done.15.refs_2_, f32[8,1024]{1,0:T(8,128)S(1)} %collective-permute-done.16.refs_3_), custom_call_target="tpu_custom_call" | custom-call | tf_op jit(solution)/shard_map/assemble/pallas_call | solution.py:296
  (5 shorter events, 0.1 us)
Async XLA Ops:
  7.7 1.9 %collective-permute-start = (f32[768,128]{1,0:T(8,128)S(1)}, f32[768,128]{1,0:T(8,128)S(1)}, u32[]{:S(2)}, u32[]{:S(2)}) collective-permute-start(f32[768,128]{1,0:T(8,128)S(1)} %get-tuple-element.30.refs_0_), channel_id=1, source_target_pairs={{0,1},{1,0},{2,3},{3,2},{4,5},{5,4},{6,7},{7,6},{8,9},{9,8},{10,11... | collective-permute-start | bytes 1179656 | tf_op jit(solution)/shard_map/ppermute | solution.py:319
  10.2 9.4 %collective-permute-start.3 = (f32[128,128]{1,0:T(8,128)S(1)}, f32[128,128]{1,0:T(8,128)S(1)}, u32[]{:S(2)}, u32[]{:S(2)}) collective-permute-start(f32[128,128]{1,0:T(8,128)S(1)} %get-tuple-element.31), channel_id=1, source_target_pairs={{0,6},{2,4},{4,2},{6,0},{8,14},{10,12},{12,10},{14,8},{16,22},{18,... | collective-permute-start | bytes 196616 | tf_op jit(solution)/shard_map/ppermute | solution.py:312
  14.0 5.5 %collective-permute-start.2 = (f32[128,128]{1,0:T(8,128)S(1)}, f32[128,128]{1,0:T(8,128)S(1)}, u32[]{:S(2)}, u32[]{:S(2)}) collective-permute-start(f32[128,128]{1,0:T(8,128)S(1)} %get-tuple-element.31), channel_id=1, source_target_pairs={{0,4},{2,6},{4,0},{6,2},{8,12},{10,14},{12,8},{14,10},{16,20},{18,... | collective-permute-start | bytes 196616 | tf_op jit(solution)/shard_map/ppermute | solution.py:312
  14.5 5.0 %collective-permute-start.1 = (f32[128,128]{1,0:T(8,128)S(1)}, f32[128,128]{1,0:T(8,128)S(1)}, u32[]{:S(2)}, u32[]{:S(2)}) collective-permute-start(f32[128,128]{1,0:T(8,128)S(1)} %get-tuple-element.31), channel_id=1, source_target_pairs={{0,2},{2,0},{4,6},{6,4},{8,10},{10,8},{12,14},{14,12},{16,18},{18,... | collective-permute-start | bytes 196616 | tf_op jit(solution)/shard_map/ppermute | solution.py:312
  16.1 13.9 %collective-permute-start.7 = (f32[128,1024]{1,0:T(8,128)S(1)}, f32[128,1024]{1,0:T(8,128)S(1)}, u32[]{:S(2)}, u32[]{:S(2)}) collective-permute-start(f32[128,1024]{1,0:T(8,128)S(1)} %get-tuple-element.35), channel_id=1, source_target_pairs={{0,2},{2,0},{4,6},{6,4},{8,10},{10,8},{12,14},{14,12},{16,18},{18,... | collective-permute-start | bytes 1572872 | tf_op jit(solution)/shard_map/ppermute | solution.py:312
  18.1 13.6 %collective-permute-start.9 = (f32[128,1024]{1,0:T(8,128)S(1)}, f32[128,1024]{1,0:T(8,128)S(1)}, u32[]{:S(2)}, u32[]{:S(2)}) collective-permute-start(f32[128,1024]{1,0:T(8,128)S(1)} %get-tuple-element.36), channel_id=1, source_target_pairs={{0,4},{2,6},{4,0},{6,2},{8,12},{10,14},{12,8},{14,10},{16,20},{18,... | collective-permute-start | bytes 1572872 | tf_op jit(solution)/shard_map/ppermute | solution.py:312
  19.6 6.1 %collective-permute-start.6 = (f32[128,128]{1,0:T(8,128)S(1)}, f32[128,128]{1,0:T(8,128)S(1)}, u32[]{:S(2)}, u32[]{:S(2)}) collective-permute-start(f32[128,128]{1,0:T(8,128)S(1)} %add_add_fusion.1), channel_id=1, source_target_pairs={{0,24},{2,26},{4,28},{6,30},{8,16},{10,18},{12,20},{14,22},{16,8},... | collective-permute-start | bytes 196616 | tf_op jit(solution)/shard_map/ppermute | solution.py:312
  23.3 5.2 %collective-permute-start.5 = (f32[128,128]{1,0:T(8,128)S(1)}, f32[128,128]{1,0:T(8,128)S(1)}, u32[]{:S(2)}, u32[]{:S(2)}) collective-permute-start(f32[128,128]{1,0:T(8,128)S(1)} %add_add_fusion.1), channel_id=1, source_target_pairs={{0,16},{2,18},{4,20},{6,22},{8,24},{10,26},{12,28},{14,30},{16,0},... | collective-permute-start | bytes 196616 | tf_op jit(solution)/shard_map/ppermute | solution.py:312
  23.3 5.2 %collective-permute-start.4 = (f32[128,128]{1,0:T(8,128)S(1)}, f32[128,128]{1,0:T(8,128)S(1)}, u32[]{:S(2)}, u32[]{:S(2)}) collective-permute-start(f32[128,128]{1,0:T(8,128)S(1)} %add_add_fusion.1), channel_id=1, source_target_pairs={{0,8},{2,10},{4,12},{6,14},{8,0},{10,2},{12,4},{14,6},{16,24},{18,... | collective-permute-start | bytes 196616 | tf_op jit(solution)/shard_map/ppermute | solution.py:312
  30.1 8.2 %collective-permute-start.8 = (f32[128,512]{1,0:T(8,128)S(1)}, f32[128,512]{1,0:T(8,128)S(1)}, u32[]{:S(2)}, u32[]{:S(2)}) collective-permute-start(f32[128,512]{1,0:T(8,128)S(1)} %onward.2), channel_id=1, source_target_pairs={{0,4},{2,6},{4,0},{6,2},{8,12},{10,14},{12,8},{14,10},{16,20},{18,... | collective-permute-start | bytes 786440 | tf_op jit(solution)/shard_map/ppermute | solution.py:312
  31.7 6.7 %collective-permute-start.10 = (f32[128,512]{1,0:T(8,128)S(1)}, f32[128,512]{1,0:T(8,128)S(1)}, u32[]{:S(2)}, u32[]{:S(2)}) collective-permute-start(f32[128,512]{1,0:T(8,128)S(1)} %onward.3), channel_id=1, source_target_pairs={{0,2},{2,0},{4,6},{6,4},{8,10},{10,8},{12,14},{14,12},{16,18},{18,... | collective-permute-start | bytes 786440 | tf_op jit(solution)/shard_map/ppermute | solution.py:312
  39.0 5.7 %collective-permute-start.11 = (f32[32,1024]{1,0:T(8,128)S(1)}, f32[32,1024]{1,0:T(8,128)S(1)}, u32[]{:S(2)}, u32[]{:S(2)}) collective-permute-start(f32[32,1024]{1,0:T(8,128)S(1)} %get-tuple-element.45), channel_id=1, source_target_pairs={{0,8},{2,10},{4,12},{6,14},{8,0},{10,2},{12,4},{14,6},{16,24},{18,... | collective-permute-start | bytes 393224 | tf_op jit(solution)/shard_map/ppermute | solution.py:312
  40.7 10.8 %collective-permute-start.12 = (f32[32,1024]{1,0:T(8,128)S(1)}, f32[32,1024]{1,0:T(8,128)S(1)}, u32[]{:S(2)}, u32[]{:S(2)}) collective-permute-start(f32[32,1024]{1,0:T(8,128)S(1)} %get-tuple-element.46), channel_id=1, source_target_pairs={{0,16},{2,18},{4,20},{6,22},{8,24},{10,26},{12,28},{14,30},{16,0},... | collective-permute-start | bytes 393224 | tf_op jit(solution)/shard_map/ppermute | solution.py:312
  43.2 8.2 %collective-permute-start.13 = (f32[32,1024]{1,0:T(8,128)S(1)}, f32[32,1024]{1,0:T(8,128)S(1)}, u32[]{:S(2)}, u32[]{:S(2)}) collective-permute-start(f32[32,1024]{1,0:T(8,128)S(1)} %get-tuple-element.47), channel_id=1, source_target_pairs={{0,24},{2,26},{4,28},{6,30},{8,16},{10,18},{12,20},{14,22},{16,8},... | collective-permute-start | bytes 393224 | tf_op jit(solution)/shard_map/ppermute | solution.py:312
  51.5 4.0 %collective-permute-start.14 = (f32[8,1024]{1,0:T(8,128)S(1)}, f32[8,1024]{1,0:T(8,128)S(1)}, u32[]{:S(2)}, u32[]{:S(2)}) collective-permute-start(f32[8,1024]{1,0:T(8,128)S(1)} %get-tuple-element.55), channel_id=1, source_target_pairs={{0,2},{2,0},{4,6},{6,4},{8,10},{10,8},{12,14},{14,12},{16,18},{18,... | collective-permute-start | bytes 98312 | tf_op jit(solution)/shard_map/ppermute | solution.py:312
  52.8 3.9 %collective-permute-start.15 = (f32[8,1024]{1,0:T(8,128)S(1)}, f32[8,1024]{1,0:T(8,128)S(1)}, u32[]{:S(2)}, u32[]{:S(2)}) collective-permute-start(f32[8,1024]{1,0:T(8,128)S(1)} %get-tuple-element.56), channel_id=1, source_target_pairs={{0,4},{2,6},{4,0},{6,2},{8,12},{10,14},{12,8},{14,10},{16,20},{18,... | collective-permute-start | bytes 98312 | tf_op jit(solution)/shard_map/ppermute | solution.py:312
  53.3 4.8 %collective-permute-start.16 = (f32[8,1024]{1,0:T(8,128)S(1)}, f32[8,1024]{1,0:T(8,128)S(1)}, u32[]{:S(2)}, u32[]{:S(2)}) collective-permute-start(f32[8,1024]{1,0:T(8,128)S(1)} %get-tuple-element.57), channel_id=1, source_target_pairs={{0,6},{2,4},{4,2},{6,0},{8,14},{10,12},{12,10},{14,8},{16,22},{18,... | collective-permute-start | bytes 98312 | tf_op jit(solution)/shard_map/ppermute | solution.py:312

commit v3 on v2

--- a/solution.py
+++ b/solution.py
@@ -12,6 +12,7 @@
 
 precise = lax.Precision.HIGHEST
 MIB = 1 << 20
+little = pl.CostEstimate(flops=1000, bytes_accessed=1000, transcendentals=0)
 
 
 def split(value):
@@ -37,18 +38,16 @@
     return pltpu.CompilerParams(vmem_limit_bytes=mib * MIB)
 
 
-def sketch_kernel(unit, gain, depth, dev_hbm, sign_hbm, high_ref, low_ref, out_ref, dev_buf, sign_buf, omega, dev_sem, sign_sem):
-    block = dev_buf.shape[1]
-    steps = high_ref.shape[0] // block
+def sketch_kernel(unit, gain, steps, depth, dev_hbm, sign_hbm, dev_ref, out_ref, sign_buf, omega, dev_sem, sign_sem):
+    block = dev_ref.shape[0] // steps
     signs = pltpu.make_async_copy(sign_hbm, sign_buf, sign_sem)
     signs.start()
 
     def fetch(i):
-        return pltpu.make_async_copy(
-            dev_hbm.at[pl.ds(i * block, block), :], dev_buf.at[i % depth], dev_sem.at[i % depth]
-        )
-
-    for i in range(min(depth - 1, steps)):
+        here = pl.ds(i * block, block)
+        return pltpu.make_async_copy(dev_hbm.at[here, :], dev_ref.at[here, :], dev_sem.at[i])
+
+    for i in range(depth - 1):
         fetch(i).start()
     signs.wait()
     omega[...] = (sign_buf[...].astype(jnp.float32) * unit).astype(jnp.bfloat16)
@@ -57,30 +56,27 @@
             fetch(i + depth - 1).start()
         fetch(i).wait()
         here = slice(i * block, (i + 1) * block)
-        high, low = split(dev_buf[i % depth])
-        high_ref[here, :] = high
-        low_ref[here, :] = low
+        high, low = split(dev_ref[here, :])
         out_ref[here, :] = (dot(high, omega[...]) + dot(low, omega[...])) * gain
 
 
 def sketch_of(dev, signs):
     rows, cols = dev.shape
     rank = signs.shape[1]
-    block, depth = rows // 4, 3
+    steps, depth = 4, 3
     unit = 2.0 ** -math.ceil(math.log2(math.sqrt(SCANS)))
     gain = 1.0 / (math.sqrt(SCANS) * unit)
     dev = pltpu.with_memory_space_constraint(dev, pltpu.HBM)
     signs = pltpu.with_memory_space_constraint(signs, pltpu.HBM)
     return pl.pallas_call(
-        functools.partial(sketch_kernel, unit, gain, depth),
+        functools.partial(sketch_kernel, unit, gain, steps, depth),
         in_specs=[pl.BlockSpec(memory_space=pltpu.HBM)] * 2,
-        out_specs=[vmem()] * 3,
-        out_shape=[pltpu.VMEM((rows, cols), jnp.bfloat16)] * 2 + [pltpu.VMEM((rows, rank), jnp.float32)],
+        out_specs=[vmem()] * 2,
+        out_shape=[pltpu.VMEM((rows, cols), jnp.float32), pltpu.VMEM((rows, rank), jnp.float32)],
         scratch_shapes=[
-            pltpu.VMEM((depth, block, cols), jnp.float32),
             pltpu.VMEM((cols, rank), jnp.int32),
             pltpu.VMEM((cols, rank), jnp.bfloat16),
-            pltpu.SemaphoreType.DMA((depth,)),
+            pltpu.SemaphoreType.DMA((steps,)),
             pltpu.SemaphoreType.DMA,
         ],
         compiler_params=params(24),
@@ -88,64 +84,88 @@
     )(dev, signs)
 
 
-def gram_kernel(parts, *refs):
-    total_ref, pair_ref, gram_ref = refs[parts:]
+def join_kernel(parts, *refs):
+    total_ref, pair_ref = refs[parts:]
     total = refs[0][...]
     for ref in refs[1:parts]:
         total = total + ref[...]
     total_ref[...] = total
-    flat = total.T
-    high, low = split(flat)
-    rank = flat.shape[0]
+    high, low = split(total.T)
+    rank = high.shape[0]
     pair_ref[:rank, :] = high
     pair_ref[rank:, :] = low
-    gram_ref[...] = lax.dot_general(
-        flat, total, (((1,), (0,)), ((), ())),
-        precision=precise, preferred_element_type=jnp.float32,
-    )
-
-
-def gram_of(*sketches):
+
+
+def join(*sketches):
     rows, rank = sketches[0].shape
     return pl.pallas_call(
-        functools.partial(gram_kernel, len(sketches)),
+        functools.partial(join_kernel, len(sketches)),
         in_specs=[vmem()] * len(sketches),
-        out_specs=[vmem()] * 3,
+        out_specs=[vmem()] * 2,
         out_shape=[
             jax.ShapeDtypeStruct((rows, rank), jnp.float32),
             jax.ShapeDtypeStruct((2 * rank, rows), jnp.bfloat16),
-            jax.ShapeDtypeStruct((rank, rank), jnp.float32),
         ],
         compiler_params=params(8),
+        name="join",
+    )(*sketches)
+
+
+def places(shape):
+    return lax.broadcasted_iota(jnp.int32, shape, 0), lax.broadcasted_iota(jnp.int32, shape, 1)
+
+
+def gram_kernel(tall_ref, packed_ref):
+    tall = tall_ref[...]
+    gram = lax.dot_general(
+        tall, tall, (((0,), (0,)), ((), ())),
+        precision=precise, preferred_element_type=jnp.float32,
+    )
+    half = gram.shape[0] // 2
+    last = pltpu.roll(gram[half:], half, 1)
+    rows, lanes = places(last.shape)
+    packed_ref[:half, :] = jnp.where(rows <= lanes, gram[:half], last)
+    diagonal = jnp.sum(jnp.where(rows == lanes, last, 0.0), axis=0, keepdims=True)
+    packed_ref[half:, :] = jnp.broadcast_to(diagonal, (8, last.shape[1]))
+
+
+def gram_of(tall):
+    rank = tall.shape[1]
+    return pl.pallas_call(
+        gram_kernel,
+        in_specs=[vmem()],
+        out_specs=vmem(),
+        out_shape=jax.ShapeDtypeStruct((rank // 2 + 8, rank), jnp.float32),
+        compiler_params=params(8),
+        cost_estimate=little,
         name="gram",
-    )(*sketches)
-
-
-def cross_kernel(block, stay, pair_ref, high_ref, low_ref, *outs):
+    )(tall)
+
+
+def cross_kernel(block, stay, pair_ref, dev_ref, *outs):
     rank, width = outs[0].shape
     x, y = place()[:2]
     chunks = (x, 2 + y) if stay else (1 - x, 3 - y)
     for chunk, out in zip(chunks, outs):
         for t in range(width // block):
             start = pl.multiple_of(chunk * width + t * block, 128)
-            high = high_ref[:, pl.ds(start, block)]
-            low = low_ref[:, pl.ds(start, block)]
+            high, low = split(dev_ref[:, pl.ds(start, block)])
             both = dot(pair_ref[...], high)
             out[:, t * block:(t + 1) * block] = (both[:rank] + both[rank:]) + dot(pair_ref[:rank, :], low)
 
 
-def cross_of(stay, pair, high, low):
+def cross_of(stay, pair, dev):
     rank, rows = pair.shape[0] // 2, pair.shape[1]
-    width = high.shape[1] // 4
+    width = dev.shape[1] // 4
     return pl.pallas_call(
         functools.partial(cross_kernel, min(512, width), stay),
-        in_specs=[vmem()] * 3,
+        in_specs=[vmem()] * 2,
         out_specs=[vmem()] * 2,
         out_shape=[jax.ShapeDtypeStruct((rank, width), jnp.float32)] * 2,
         compiler_params=params(8),
-        cost_estimate=pl.CostEstimate(flops=12 * rank * rows * width, bytes_accessed=8 * rows * width, transcendentals=0),
+        cost_estimate=little,
         name="cross_stay" if stay else "cross_leave",
-    )(pair, high, low)
+    )(pair, dev)
 
 
 def thirds(value):
@@ -156,11 +176,17 @@
     return high, middle, low
 
 
-def inverse_kernel(gram_ref, out_ref, work):
-    rank = gram_ref.shape[0]
-    rows = lax.broadcasted_iota(jnp.int32, (rank, rank), 0)
-    lanes = lax.broadcasted_iota(jnp.int32, (rank, rank), 1)
-    work[:, :rank] = gram_ref[...]
+def inverse_kernel(packed_ref, out_ref, work):
+    rank = packed_ref.shape[1]
+    half = rank // 2
+    packed = packed_ref[:half, :]
+    rows, lanes = places(packed.shape)
+    corner = jnp.where(lanes < half, packed, 0.0)
+    turned = jnp.concatenate([corner, jnp.zeros_like(corner)], axis=0).T[:half]
+    work[:half, :rank] = jnp.where(rows <= lanes, packed, turned)
+    last = jnp.where(rows > lanes, packed, jnp.where(rows < lanes, turned, packed_ref[half:half + 1, :]))
+    work[half:, :rank] = jnp.where(lanes < half, 0.0, pltpu.roll(last, half, 1))
+    rows, lanes = places((rank, rank))
     work[:, rank:] = jnp.where(rows == lanes, 1.0, 0.0)
     for base in range(0, rank, 8):
         left = work[base:base + 8, :rank]
@@ -194,8 +220,8 @@
     out_ref[...] = jnp.where(lanes <= rows, work[:, rank:], 0.0)
 
 
-def inverse_of(gram):
-    rank = gram.shape[0]
+def inverse_of(packed):
+    rank = packed.shape[1]
     return pl.pallas_call(
         inverse_kernel,
         in_specs=[vmem()],
@@ -203,9 +229,9 @@
         out_shape=jax.ShapeDtypeStruct((rank, rank), jnp.float32),
         scratch_shapes=[pltpu.VMEM((rank, 2 * rank), jnp.float32)],
         compiler_params=params(8),
-        cost_estimate=pl.CostEstimate(flops=8 * 10**9, bytes_accessed=10**6, transcendentals=0),
+        cost_estimate=little,
         name="inverse",
-    )(gram)
+    )(packed)
 
 
 def onward_kernel(axis, keep_ref, got_ref, out_ref):
@@ -311,25 +337,25 @@
     def swap(value, bit):
         return lax.ppermute(value, "rows", [(i, i ^ bit) for i in range(n)])
 
-    high, low, part = sketch_of(deviations, test_signs)
+    kept, part = sketch_of(deviations, test_signs)
     step = 1
     while 2 * step < n_cols:
         part = part + lax.ppermute(part, "cols", [(i, i ^ step) for i in range(n_cols)])
         step *= 2
     other = lax.ppermute(part, "cols", [(i, i ^ step) for i in range(n_cols)])
-    sketch, pair, gram = gram_of(part, other)
-
-    leave = cross_of(False, pair, high, low)
-    stay = cross_of(True, pair, high, low)
-
-    step, beside = 1, [leave, stay]
-    while step < n:
+    sketch, pair = join(part, other)
+
+    leave = cross_of(False, pair, kept)
+    stay = cross_of(True, pair, kept)
+
+    gram = gram_of(lax.optimization_barrier((sketch, leave))[0])
+    steps, beside = [4 ** i for i in range(1, n) if 4 ** i < n] + [1], [stay]
+    for step in steps:
         found = [swap(gram, step * k) for k in range(1, min(4, n // step))]
         if beside:
-            found, _ = lax.optimization_barrier((found, beside.pop(0)))
+            found, _ = lax.optimization_barrier((found, beside.pop()))
         for value in found:
             gram = gram + value
-        step *= 4
     inverse = inverse_of(gram)
 
     got_x, got_y = swap(leave[0], 1), swap(leave[1], 2)

time: 58.9 us -> 56.7 us (0.963)
  waiting for transfers between devices: 15.8 us -> 14.3 us
  starting transfers between devices: 23.8 us -> 23.2 us
    ppermute x16, waiting for transfers between devices: 14.4 us -> 13 us  [swap(): return lax.ppermute(value, 'rows', [(i, i ^ bit) for i in range(n)])]
    ppermute x16, starting transfers between devices: 23.2 us -> 22.6 us  [swap(): return lax.ppermute(value, 'rows', [(i, i ^ bit) for i in range(n)])]
    pallas_call x2 -> x3, Pallas kernels: 7.64 us -> 7.47 us  [the longest x1 6.7 us: sketch_of(): pl.pallas_call(functools.partial(sketch_kernel, unit, gain, steps, depth)...]
  transfers between devices with their start and end apart: 17 -> 17, of which waited for: 9 -> 8; matrix products, arithmetic and copies ran while one was open for 2% -> 2% of each run, Pallas kernels for 14% -> 13%
where the time goes in v3:
time: 56.7 us; the launch traced here: 56.6 us
  starting transfers between devices  23.2 us (41%)
  Pallas kernels  17.2 us (30%)
  waiting for transfers between devices  14.3 us (25%)
  matrix products  1.23 us (2%)
  between operations  0.72 us (1%)
    ppermute x16, starting transfers between devices, swap(): return lax.ppermute(value, 'rows', [(i, i ^ bit) for i in range(n)])  22.6 us
    ppermute x16, waiting for transfers between devices, swap(): return lax.ppermute(value, 'rows', [(i, i ^ bit) for i in range(n)])  13 us
    pallas_call x1, Pallas kernels, sketch_of(): pl.pallas_call(functools.partial(sketch_kernel, unit, gain, steps, depth)...  6.7 us
    pallas_call x1, Pallas kernels, inverse_of(): pl.pallas_call(inverse_kernel, in_specs=[vmem()], out_specs=vmem(), out_s...  5.45 us
    pallas_call x2, Pallas kernels, cross_of(): pl.pallas_call(functools.partial(cross_kernel, min(512, width), stay), in...  2.86 us
    ppermute x1, waiting for transfers between devices, local(): other = lax.ppermute(part, 'cols', [(i, i ^ step) for i in range(n_cols)])  1.35 us
    dot_general x1, matrix products, local(): lax.dot_general(sketch, inverse, (((1,), (1,)), ((), ())), precision=prec...  1.23 us
  transfers between devices with their start and end apart: 17, of which 8 were waited for; matrix products, arithmetic and copies ran while one was open for 2% of the time, Pallas kernels for 13%

profile of v3, /device:TPU:0, one launch (start us, length us, event | category | flops | bytes accessed | tf_op | source)
XLA Modules:
  0.0 56.6 jit_solution(6030459549481004728)
XLA Ops:
  0.6 6.7 %sketch.1 = (f32[768,4096]{1,0:T(8,128)S(1)}, f32[768,128]{1,0:T(8,128)S(1)}) custom-call(f32[768,4096]{1,0:T(8,128)} %dev_hbm.1, s32[4096,128]{1,0:T(8,128)} %sign_hbm.1), custom_call_target="tpu_custom_call" | custom-call | tf_op jit(solution)/shard_map/sketch/pallas_call | solution.py:71
  7.3 0.5 collective-permute-start
  7.9 1.3 %collective-permute-done.refs_1_ = f32[768,128]{1,0:T(8,128)S(1)} collective-permute-done((f32[768,128]{1,0:T(8,128)S(1)}, f32[768,128]{1,0:T(8,128)S(1)}, u32[]{:S(2)}, u32[]{:S(2)}) %collective-permute-start) | collective-permute-done | bytes 393248 | tf_op jit(solution)/shard_map/ppermute | solution.py:345
  9.2 0.2 join.1
  9.4 1.4 %cross_leave.1 = (f32[128,1024]{1,0:T(8,128)S(1)}, f32[128,1024]{1,0:T(8,128)S(1)}) custom-call(bf16[256,768]{1,0:T(8,128)(2,1)S(1)} %get-tuple-element.28.pair_ref, f32[768,4096]{1,0:T(8,128)S(1)} %get-tuple-element.29.dev_ref), custom_call_target="tpu_custom_call" | custom-call | flops 1000 | bytes 1000 | tf_op jit(solution)/shard_map/cross_leave/pallas_call | solution.py:160
  10.8 2.9 %collective-permute-start.7 = (f32[128,1024]{1,0:T(8,128)S(1)}, f32[128,1024]{1,0:T(8,128)S(1)}, u32[]{:S(2)}, u32[]{:S(2)}) collective-permute-start(f32[128,1024]{1,0:T(8,128)S(1)} %get-tuple-element.30), channel_id=1, source_target_pairs={{0,2},{2,0},{4,6},{6,4},{8,10},{10,8},{12,14},{14,12},{16,18},{18,... | collective-permute-start | bytes 1572872 | tf_op jit(solution)/shard_map/ppermute | solution.py:338
  13.8 1.5 %collective-permute-start.9 = (f32[128,1024]{1,0:T(8,128)S(1)}, f32[128,1024]{1,0:T(8,128)S(1)}, u32[]{:S(2)}, u32[]{:S(2)}) collective-permute-start(f32[128,1024]{1,0:T(8,128)S(1)} %get-tuple-element.31), channel_id=1, source_target_pairs={{0,4},{2,6},{4,0},{6,2},{8,12},{10,14},{12,8},{14,10},{16,20},{18,... | collective-permute-start | bytes 1572872 | tf_op jit(solution)/shard_map/ppermute | solution.py:338
  15.3 0.6 %gram.1 = f32[72,128]{1,0:T(8,128)S(1)} custom-call(f32[768,128]{1,0:T(8,128)S(1)} %get-tuple-element.32.tall_ref), custom_call_target="tpu_custom_call" | custom-call | flops 1000 | bytes 1000 | tf_op jit(solution)/shard_map/gram/pallas_call | solution.py:134
  15.9 3.7 %collective-permute-start.3 = (f32[72,128]{1,0:T(8,128)S(1)}, f32[72,128]{1,0:T(8,128)S(1)}, u32[]{:S(2)}, u32[]{:S(2)}) collective-permute-start(f32[72,128]{1,0:T(8,128)S(1)} %gram.1), channel_id=1, source_target_pairs={{0,24},{2,26},{4,28},{6,30},{8,16},{10,18},{12,20},{14,22},{16,8},... | collective-permute-start | bytes 110600 | tf_op jit(solution)/shard_map/ppermute | solution.py:338
  19.5 0.0 collective-permute-start.2
  19.5 0.8 %collective-permute-start.1 = (f32[72,128]{1,0:T(8,128)S(1)}, f32[72,128]{1,0:T(8,128)S(1)}, u32[]{:S(2)}, u32[]{:S(2)}) collective-permute-start(f32[72,128]{1,0:T(8,128)S(1)} %gram.1), channel_id=1, source_target_pairs={{0,8},{2,10},{4,12},{6,14},{8,0},{10,2},{12,4},{14,6},{16,24},{18,... | collective-permute-start | bytes 110600 | tf_op jit(solution)/shard_map/ppermute | solution.py:338
  20.3 1.4 %cross_stay.1 = (f32[128,1024]{1,0:T(8,128)S(1)}, f32[128,1024]{1,0:T(8,128)S(1)}) custom-call(bf16[256,768]{1,0:T(8,128)(2,1)S(1)} %get-tuple-element.28.pair_ref, f32[768,4096]{1,0:T(8,128)S(1)} %get-tuple-element.29.dev_ref), custom_call_target="tpu_custom_call" | custom-call | flops 1000 | bytes 1000 | tf_op jit(solution)/shard_map/cross_stay/pallas_call | solution.py:160
  21.8 0.3 collective-permute-done.3
  22.1 2.3 %collective-permute-done.2 = f32[72,128]{1,0:T(8,128)S(1)} collective-permute-done((f32[72,128]{1,0:T(8,128)S(1)}, f32[72,128]{1,0:T(8,128)S(1)}, u32[]{:S(2)}, u32[]{:S(2)}) %collective-permute-start.2) | collective-permute-done | bytes 36896 | tf_op jit(solution)/shard_map/ppermute | solution.py:338
  24.4 0.0 collective-permute-done.1
  24.4 0.5 collective-permute-start.6
  25.0 1.5 %collective-permute-start.5 = (f32[72,128]{1,0:T(8,128)S(1)}, f32[72,128]{1,0:T(8,128)S(1)}, u32[]{:S(2)}, u32[]{:S(2)}) collective-permute-start(f32[72,128]{1,0:T(8,128)S(1)} %add_add_fusion.1), channel_id=1, source_target_pairs={{0,4},{2,6},{4,0},{6,2},{8,12},{10,14},{12,8},{14,10},{16,20},{18,... | collective-permute-start | bytes 110600 | tf_op jit(solution)/shard_map/ppermute | solution.py:338
  26.5 1.5 %collective-permute-start.4 = (f32[72,128]{1,0:T(8,128)S(1)}, f32[72,128]{1,0:T(8,128)S(1)}, u32[]{:S(2)}, u32[]{:S(2)}) collective-permute-start(f32[72,128]{1,0:T(8,128)S(1)} %add_add_fusion.1), channel_id=1, source_target_pairs={{0,2},{2,0},{4,6},{6,4},{8,10},{10,8},{12,14},{14,12},{16,18},{18,... | collective-permute-start | bytes 110600 | tf_op jit(solution)/shard_map/ppermute | solution.py:338
  28.0 0.0 collective-permute-done.7.got_ref.got_x
  28.0 0.6 %collective-permute-start.8 = (f32[128,512]{1,0:T(8,128)S(1)}, f32[128,512]{1,0:T(8,128)S(1)}, u32[]{:S(2)}, u32[]{:S(2)}) collective-permute-start(f32[128,512]{1,0:T(8,128)S(1)} %onward.2), channel_id=1, source_target_pairs={{0,4},{2,6},{4,0},{6,2},{8,12},{10,14},{12,8},{14,10},{16,20},{18,... | collective-permute-start | bytes 786440 | tf_op jit(solution)/shard_map/ppermute | solution.py:338
  28.6 0.0 collective-permute-done.9.got_ref.got_y
  28.7 1.6 %collective-permute-start.10 = (f32[128,512]{1,0:T(8,128)S(1)}, f32[128,512]{1,0:T(8,128)S(1)}, u32[]{:S(2)}, u32[]{:S(2)}) collective-permute-start(f32[128,512]{1,0:T(8,128)S(1)} %onward.3), channel_id=1, source_target_pairs={{0,2},{2,0},{4,6},{6,4},{8,10},{10,8},{12,14},{14,12},{16,18},{18,... | collective-permute-start | bytes 786440 | tf_op jit(solution)/shard_map/ppermute | solution.py:338
  30.2 0.0 collective-permute-done.6
  30.2 0.0 collective-permute-done.5
  30.2 0.5 collective-permute-done.4
  30.8 5.5 %inverse.1.inverse_ref = f32[128,128]{1,0:T(8,128)S(1)} custom-call(f32[72,128]{1,0:T(8,128)S(1)} %add_add_fusion.packed_ref), custom_call_target="tpu_custom_call" | custom-call | flops 1000 | bytes 1000 | tf_op jit(solution)/shard_map/inverse/pallas_call | solution.py:225
  36.2 0.0 collective-permute-done.8.then_x
  36.2 0.0 collective-permute-done.10.then_y
  36.2 0.6 %project.1 = (f32[32,1024]{1,0:T(8,128)S(1)}, f32[32,1024]{1,0:T(8,128)S(1)}, f32[32,1024]{1,0:T(8,128)S(1)}, f32[32,1024]{1,0:T(8,128)S(1)}) custom-call(f32[128,128]{1,0:T(8,128)S(1)} %inverse.1.inverse_ref, f32[128,1024]{1,0:T(8,128)S(1)} %get-tuple-element.33.keep_ref.keep_x, f32[128,1024]{1,0:T(8,128)S(1)} %collective-permute-done.7.got_ref.got_x, ...), custom_call_target="tpu_custom_call" | custom-call | tf_op jit(solution)/shard_map/project/pallas_call | solution.py:277
  36.8 1.1 %collective-permute-start.11 = (f32[32,1024]{1,0:T(8,128)S(1)}, f32[32,1024]{1,0:T(8,128)S(1)}, u32[]{:S(2)}, u32[]{:S(2)}) collective-permute-start(f32[32,1024]{1,0:T(8,128)S(1)} %get-tuple-element.38), channel_id=1, source_target_pairs={{0,8},{2,10},{4,12},{6,14},{8,0},{10,2},{12,4},{14,6},{16,24},{18,... | collective-permute-start | bytes 393224 | tf_op jit(solution)/shard_map/ppermute | solution.py:338
  38.0 2.6 %collective-permute-start.12 = (f32[32,1024]{1,0:T(8,128)S(1)}, f32[32,1024]{1,0:T(8,128)S(1)}, u32[]{:S(2)}, u32[]{:S(2)}) collective-permute-start(f32[32,1024]{1,0:T(8,128)S(1)} %get-tuple-element.39), channel_id=1, source_target_pairs={{0,16},{2,18},{4,20},{6,22},{8,24},{10,26},{12,28},{14,30},{16,0},... | collective-permute-start | bytes 393224 | tf_op jit(solution)/shard_map/ppermute | solution.py:338
  40.6 0.7 %collective-permute-start.13 = (f32[32,1024]{1,0:T(8,128)S(1)}, f32[32,1024]{1,0:T(8,128)S(1)}, u32[]{:S(2)}, u32[]{:S(2)}) collective-permute-start(f32[32,1024]{1,0:T(8,128)S(1)} %get-tuple-element.40), channel_id=1, source_target_pairs={{0,24},{2,26},{4,28},{6,30},{8,16},{10,18},{12,20},{14,22},{16,8},... | collective-permute-start | bytes 393224 | tf_op jit(solution)/shard_map/ppermute | solution.py:338
  41.3 1.2 %convolution_multiply_fusion = f32[768,128]{1,0:T(8,128)} fusion(f32[768,128]{1,0:T(8,128)S(1)} %get-tuple-element.32.tall_ref, f32[128,128]{1,0:T(8,128)S(1)} %inverse.1.inverse_ref), kind=kOutput, calls=%fused_computation | convolution fusion | flops 151093248 | bytes 851968 | tf_op jit(solution)/shard_map/dot_general | solution.py:366
  42.5 0.0 collective-permute-done.11.refs_1_
  42.5 6.4 %collective-permute-done.12.refs_2_ = f32[32,1024]{1,0:T(8,128)S(1)} collective-permute-done((f32[32,1024]{1,0:T(8,128)S(1)}, f32[32,1024]{1,0:T(8,128)S(1)}, u32[]{:S(2)}, u32[]{:S(2)}) %collective-permute-start.12) | collective-permute-done | bytes 131104 | tf_op jit(solution)/shard_map/ppermute | solution.py:338
  49.0 0.0 collective-permute-done.13.refs_3_
  49.0 0.8 %collective-permute-start.14 = (f32[8,1024]{1,0:T(8,128)S(1)}, f32[8,1024]{1,0:T(8,128)S(1)}, u32[]{:S(2)}, u32[]{:S(2)}) collective-permute-start(f32[8,1024]{1,0:T(8,128)S(1)} %get-tuple-element.47), channel_id=1, source_target_pairs={{0,2},{2,0},{4,6},{6,4},{8,10},{10,8},{12,14},{14,12},{16,18},{18,... | collective-permute-start | bytes 98312 | tf_op jit(solution)/shard_map/ppermute | solution.py:338
  49.8 1.3 %collective-permute-start.15 = (f32[8,1024]{1,0:T(8,128)S(1)}, f32[8,1024]{1,0:T(8,128)S(1)}, u32[]{:S(2)}, u32[]{:S(2)}) collective-permute-start(f32[8,1024]{1,0:T(8,128)S(1)} %get-tuple-element.48), channel_id=1, source_target_pairs={{0,4},{2,6},{4,0},{6,2},{8,12},{10,14},{12,8},{14,10},{16,20},{18,... | collective-permute-start | bytes 98312 | tf_op jit(solution)/shard_map/ppermute | solution.py:338
  51.1 1.5 %collective-permute-start.16 = (f32[8,1024]{1,0:T(8,128)S(1)}, f32[8,1024]{1,0:T(8,128)S(1)}, u32[]{:S(2)}, u32[]{:S(2)}) collective-permute-start(f32[8,1024]{1,0:T(8,128)S(1)} %get-tuple-element.49), channel_id=1, source_target_pairs={{0,6},{2,4},{4,2},{6,0},{8,14},{10,12},{12,10},{14,8},{16,22},{18,... | collective-permute-start | bytes 98312 | tf_op jit(solution)/shard_map/ppermute | solution.py:338
  52.6 0.4 collective-permute-done.14.refs_1_
  53.0 0.7 %collective-permute-done.15.refs_2_ = f32[8,1024]{1,0:T(8,128)S(1)} collective-permute-done((f32[8,1024]{1,0:T(8,128)S(1)}, f32[8,1024]{1,0:T(8,128)S(1)}, u32[]{:S(2)}, u32[]{:S(2)}) %collective-permute-start.15) | collective-permute-done | bytes 32800 | tf_op jit(solution)/shard_map/ppermute | solution.py:338
  53.7 2.2 %collective-permute-done.16.refs_3_ = f32[8,1024]{1,0:T(8,128)S(1)} collective-permute-done((f32[8,1024]{1,0:T(8,128)S(1)}, f32[8,1024]{1,0:T(8,128)S(1)}, u32[]{:S(2)}, u32[]{:S(2)}) %collective-permute-start.16) | collective-permute-done | bytes 32800 | tf_op jit(solution)/shard_map/ppermute | solution.py:338
  55.9 0.7 %assemble.1 = f32[8,4096]{1,0:T(8,128)} custom-call(f32[8,1024]{1,0:T(8,128)S(1)} %get-tuple-element.46.refs_0_, f32[8,1024]{1,0:T(8,128)S(1)} %collective-permute-done.14.refs_1_, f32[8,1024]{1,0:T(8,128)S(1)} %collective-permute-done.15.refs_2_, f32[8,1024]{1,0:T(8,128)S(1)} %collective-permute-done.16.refs_3_), custom_call_target="tpu_custom_call" | custom-call | tf_op jit(solution)/shard_map/assemble/pallas_call | solution.py:322
  (5 shorter events, 0.1 us)
Async XLA Ops:
  7.3 1.9 %collective-permute-start = (f32[768,128]{1,0:T(8,128)S(1)}, f32[768,128]{1,0:T(8,128)S(1)}, u32[]{:S(2)}, u32[]{:S(2)}) collective-permute-start(f32[768,128]{1,0:T(8,128)S(1)} %get-tuple-element.26.refs_0_), channel_id=1, source_target_pairs={{0,1},{1,0},{2,3},{3,2},{4,5},{5,4},{6,7},{7,6},{8,9},{9,8},{10,11... | collective-permute-start | bytes 1179656 | tf_op jit(solution)/shard_map/ppermute | solution.py:345
  10.8 17.1 %collective-permute-start.7 = (f32[128,1024]{1,0:T(8,128)S(1)}, f32[128,1024]{1,0:T(8,128)S(1)}, u32[]{:S(2)}, u32[]{:S(2)}) collective-permute-start(f32[128,1024]{1,0:T(8,128)S(1)} %get-tuple-element.30), channel_id=1, source_target_pairs={{0,2},{2,0},{4,6},{6,4},{8,10},{10,8},{12,14},{14,12},{16,18},{18,... | collective-permute-start | bytes 1572872 | tf_op jit(solution)/shard_map/ppermute | solution.py:338
  13.8 14.9 %collective-permute-start.9 = (f32[128,1024]{1,0:T(8,128)S(1)}, f32[128,1024]{1,0:T(8,128)S(1)}, u32[]{:S(2)}, u32[]{:S(2)}) collective-permute-start(f32[128,1024]{1,0:T(8,128)S(1)} %get-tuple-element.31), channel_id=1, source_target_pairs={{0,4},{2,6},{4,0},{6,2},{8,12},{10,14},{12,8},{14,10},{16,20},{18,... | collective-permute-start | bytes 1572872 | tf_op jit(solution)/shard_map/ppermute | solution.py:338
  15.9 6.2 %collective-permute-start.3 = (f32[72,128]{1,0:T(8,128)S(1)}, f32[72,128]{1,0:T(8,128)S(1)}, u32[]{:S(2)}, u32[]{:S(2)}) collective-permute-start(f32[72,128]{1,0:T(8,128)S(1)} %gram.1), channel_id=1, source_target_pairs={{0,24},{2,26},{4,28},{6,30},{8,16},{10,18},{12,20},{14,22},{16,8},... | collective-permute-start | bytes 110600 | tf_op jit(solution)/shard_map/ppermute | solution.py:338
  19.5 4.9 %collective-permute-start.2 = (f32[72,128]{1,0:T(8,128)S(1)}, f32[72,128]{1,0:T(8,128)S(1)}, u32[]{:S(2)}, u32[]{:S(2)}) collective-permute-start(f32[72,128]{1,0:T(8,128)S(1)} %gram.1), channel_id=1, source_target_pairs={{0,16},{2,18},{4,20},{6,22},{8,24},{10,26},{12,28},{14,30},{16,0},... | collective-permute-start | bytes 110600 | tf_op jit(solution)/shard_map/ppermute | solution.py:338
  19.5 4.9 %collective-permute-start.1 = (f32[72,128]{1,0:T(8,128)S(1)}, f32[72,128]{1,0:T(8,128)S(1)}, u32[]{:S(2)}, u32[]{:S(2)}) collective-permute-start(f32[72,128]{1,0:T(8,128)S(1)} %gram.1), channel_id=1, source_target_pairs={{0,8},{2,10},{4,12},{6,14},{8,0},{10,2},{12,4},{14,6},{16,24},{18,... | collective-permute-start | bytes 110600 | tf_op jit(solution)/shard_map/ppermute | solution.py:338
  24.4 5.8 %collective-permute-start.6 = (f32[72,128]{1,0:T(8,128)S(1)}, f32[72,128]{1,0:T(8,128)S(1)}, u32[]{:S(2)}, u32[]{:S(2)}) collective-permute-start(f32[72,128]{1,0:T(8,128)S(1)} %add_add_fusion.1), channel_id=1, source_target_pairs={{0,6},{2,4},{4,2},{6,0},{8,14},{10,12},{12,10},{14,8},{16,22},{18,... | collective-permute-start | bytes 110600 | tf_op jit(solution)/shard_map/ppermute | solution.py:338
  25.0 5.3 %collective-permute-start.5 = (f32[72,128]{1,0:T(8,128)S(1)}, f32[72,128]{1,0:T(8,128)S(1)}, u32[]{:S(2)}, u32[]{:S(2)}) collective-permute-start(f32[72,128]{1,0:T(8,128)S(1)} %add_add_fusion.1), channel_id=1, source_target_pairs={{0,4},{2,6},{4,0},{6,2},{8,12},{10,14},{12,8},{14,10},{16,20},{18,... | collective-permute-start | bytes 110600 | tf_op jit(solution)/shard_map/ppermute | solution.py:338
  26.5 4.3 %collective-permute-start.4 = (f32[72,128]{1,0:T(8,128)S(1)}, f32[72,128]{1,0:T(8,128)S(1)}, u32[]{:S(2)}, u32[]{:S(2)}) collective-permute-start(f32[72,128]{1,0:T(8,128)S(1)} %add_add_fusion.1), channel_id=1, source_target_pairs={{0,2},{2,0},{4,6},{6,4},{8,10},{10,8},{12,14},{14,12},{16,18},{18,... | collective-permute-start | bytes 110600 | tf_op jit(solution)/shard_map/ppermute | solution.py:338
  28.0 8.2 %collective-permute-start.8 = (f32[128,512]{1,0:T(8,128)S(1)}, f32[128,512]{1,0:T(8,128)S(1)}, u32[]{:S(2)}, u32[]{:S(2)}) collective-permute-start(f32[128,512]{1,0:T(8,128)S(1)} %onward.2), channel_id=1, source_target_pairs={{0,4},{2,6},{4,0},{6,2},{8,12},{10,14},{12,8},{14,10},{16,20},{18,... | collective-permute-start | bytes 786440 | tf_op jit(solution)/shard_map/ppermute | solution.py:338
  28.7 7.6 %collective-permute-start.10 = (f32[128,512]{1,0:T(8,128)S(1)}, f32[128,512]{1,0:T(8,128)S(1)}, u32[]{:S(2)}, u32[]{:S(2)}) collective-permute-start(f32[128,512]{1,0:T(8,128)S(1)} %onward.3), channel_id=1, source_target_pairs={{0,2},{2,0},{4,6},{6,4},{8,10},{10,8},{12,14},{14,12},{16,18},{18,... | collective-permute-start | bytes 786440 | tf_op jit(solution)/shard_map/ppermute | solution.py:338
  36.8 5.7 %collective-permute-start.11 = (f32[32,1024]{1,0:T(8,128)S(1)}, f32[32,1024]{1,0:T(8,128)S(1)}, u32[]{:S(2)}, u32[]{:S(2)}) collective-permute-start(f32[32,1024]{1,0:T(8,128)S(1)} %get-tuple-element.38), channel_id=1, source_target_pairs={{0,8},{2,10},{4,12},{6,14},{8,0},{10,2},{12,4},{14,6},{16,24},{18,... | collective-permute-start | bytes 393224 | tf_op jit(solution)/shard_map/ppermute | solution.py:338
  38.0 11.0 %collective-permute-start.12 = (f32[32,1024]{1,0:T(8,128)S(1)}, f32[32,1024]{1,0:T(8,128)S(1)}, u32[]{:S(2)}, u32[]{:S(2)}) collective-permute-start(f32[32,1024]{1,0:T(8,128)S(1)} %get-tuple-element.39), channel_id=1, source_target_pairs={{0,16},{2,18},{4,20},{6,22},{8,24},{10,26},{12,28},{14,30},{16,0},... | collective-permute-start | bytes 393224 | tf_op jit(solution)/shard_map/ppermute | solution.py:338
  40.6 8.4 %collective-permute-start.13 = (f32[32,1024]{1,0:T(8,128)S(1)}, f32[32,1024]{1,0:T(8,128)S(1)}, u32[]{:S(2)}, u32[]{:S(2)}) collective-permute-start(f32[32,1024]{1,0:T(8,128)S(1)} %get-tuple-element.40), channel_id=1, source_target_pairs={{0,24},{2,26},{4,28},{6,30},{8,16},{10,18},{12,20},{14,22},{16,8},... | collective-permute-start | bytes 393224 | tf_op jit(solution)/shard_map/ppermute | solution.py:338
  49.0 4.0 %collective-permute-start.14 = (f32[8,1024]{1,0:T(8,128)S(1)}, f32[8,1024]{1,0:T(8,128)S(1)}, u32[]{:S(2)}, u32[]{:S(2)}) collective-permute-start(f32[8,1024]{1,0:T(8,128)S(1)} %get-tuple-element.47), channel_id=1, source_target_pairs={{0,2},{2,0},{4,6},{6,4},{8,10},{10,8},{12,14},{14,12},{16,18},{18,... | collective-permute-start | bytes 98312 | tf_op jit(solution)/shard_map/ppermute | solution.py:338
  49.8 3.9 %collective-permute-start.15 = (f32[8,1024]{1,0:T(8,128)S(1)}, f32[8,1024]{1,0:T(8,128)S(1)}, u32[]{:S(2)}, u32[]{:S(2)}) collective-permute-start(f32[8,1024]{1,0:T(8,128)S(1)} %get-tuple-element.48), channel_id=1, source_target_pairs={{0,4},{2,6},{4,0},{6,2},{8,12},{10,14},{12,8},{14,10},{16,20},{18,... | collective-permute-start | bytes 98312 | tf_op jit(solution)/shard_map/ppermute | solution.py:338
  51.1 4.8 %collective-permute-start.16 = (f32[8,1024]{1,0:T(8,128)S(1)}, f32[8,1024]{1,0:T(8,128)S(1)}, u32[]{:S(2)}, u32[]{:S(2)}) collective-permute-start(f32[8,1024]{1,0:T(8,128)S(1)} %get-tuple-element.49), channel_id=1, source_target_pairs={{0,6},{2,4},{4,2},{6,0},{8,14},{10,12},{12,10},{14,8},{16,22},{18,... | collective-permute-start | bytes 98312 | tf_op jit(solution)/shard_map/ppermute | solution.py:338

commit v4 on v3

--- a/solution.py
+++ b/solution.py
@@ -115,13 +115,13 @@
     return lax.broadcasted_iota(jnp.int32, shape, 0), lax.broadcasted_iota(jnp.int32, shape, 1)
 
 
-def gram_kernel(tall_ref, packed_ref):
-    tall = tall_ref[...]
-    gram = lax.dot_general(
-        tall, tall, (((0,), (0,)), ((), ())),
-        precision=precise, preferred_element_type=jnp.float32,
+def gram_kernel(pair_ref, packed_ref):
+    four = lax.dot_general(
+        pair_ref[...], pair_ref[...], (((1,), (1,)), ((), ())), preferred_element_type=jnp.float32
     )
-    half = gram.shape[0] // 2
+    rank = four.shape[0] // 2
+    gram = (four[:rank, :rank] + four[rank:, rank:]) + (four[:rank, rank:] + four[rank:, :rank])
+    half = rank // 2
     last = pltpu.roll(gram[half:], half, 1)
     rows, lanes = places(last.shape)
     packed_ref[:half, :] = jnp.where(rows <= lanes, gram[:half], last)
@@ -129,8 +129,8 @@
     packed_ref[half:, :] = jnp.broadcast_to(diagonal, (8, last.shape[1]))
 
 
-def gram_of(tall):
-    rank = tall.shape[1]
+def gram_of(pair):
+    rank = pair.shape[0] // 2
     return pl.pallas_call(
         gram_kernel,
         in_specs=[vmem()],
@@ -139,7 +139,7 @@
         compiler_params=params(8),
         cost_estimate=little,
         name="gram",
-    )(tall)
+    )(pair)
 
 
 def cross_kernel(block, stay, pair_ref, dev_ref, *outs):
@@ -263,8 +263,14 @@
     at_y = pl.ds(pl.multiple_of(x * half, 128), half)
     left = (keep_x[:, at_x] + got_x[:, at_x]) + then_x[...]
     right = (keep_y[:, at_y] + got_y[:, at_y]) + then_y[...]
-    left = jnp.dot(ordered[...], left, precision=precise, preferred_element_type=jnp.float32)
-    right = jnp.dot(ordered[...], right, precision=precise, preferred_element_type=jnp.float32)
+    factor_high, factor_low = split(ordered[...])
+    factor = jnp.concatenate([factor_high, factor_high, factor_low], axis=1)
+
+    def applied(value):
+        high, low = split(value)
+        return dot(factor, jnp.concatenate([high, low, high], axis=0))
+
+    left, right = applied(left), applied(right)
     for k, out in enumerate(outs):
         out[:, :half] = left[k * group:(k + 1) * group]
         out[:, half:] = right[k * group:(k + 1) * group]
@@ -348,7 +354,7 @@
     leave = cross_of(False, pair, kept)
     stay = cross_of(True, pair, kept)
 
-    gram = gram_of(lax.optimization_barrier((sketch, leave))[0])
+    gram = gram_of(lax.optimization_barrier((pair, leave))[0])
     steps, beside = [4 ** i for i in range(1, n) if 4 ** i < n] + [1], [stay]
     for step in steps:
         found = [swap(gram, step * k) for k in range(1, min(4, n // step))]
@@ -367,12 +373,13 @@
         sketch, inverse, (((1,), (1,)), ((), ())),
         precision=precise, preferred_element_type=jnp.float32,
     ) * math.sqrt(samples)
-    found = [swap(groups[k], 4 * k) for k in range(1, n // 4)]
+    order = sorted(range(1, n // 4), key=lambda k: (k == 1, k))
+    found = [swap(groups[k], 4 * k) for k in order]
     found, basis = lax.optimization_barrier((found, basis))
 
     blocks = collect(groups[0], *found)
-    blocks = [blocks[0]] + [swap(blocks[k], k) for k in range(1, 4)]
-    return (basis, assemble(*blocks))
+    moved = lax.optimization_barrier([swap(blocks[k], k) for k in (3, 2, 1)])
+    return (basis, assemble(blocks[0], *moved[::-1]))
 
 
 def solution(mesh):

time: 56.7 us -> 54.8 us (0.966)
  waiting for transfers between devices: 14.3 us -> 13.3 us
    ppermute x16, waiting for transfers between devices: 13 us -> 11.9 us  [swap(): return lax.ppermute(value, 'rows', [(i, i ^ bit) for i in range(n)])]
  transfers between devices with their start and end apart: 17 -> 17, of which waited for: 8 -> 9; matrix products, arithmetic and copies ran while one was open for 2% -> 2% of each run, Pallas kernels for 13% -> 13%
where the time goes in v4:
time: 54.8 us; the launch traced here: 54.7 us
  starting transfers between devices  22.8 us (42%)
  Pallas kernels  16.7 us (30%)
  waiting for transfers between devices  13.3 us (24%)
  matrix products  1.22 us (2%)
  between operations  0.71 us (1%)
    ppermute x16, starting transfers between devices, swap(): return lax.ppermute(value, 'rows', [(i, i ^ bit) for i in range(n)])  22.3 us
    ppermute x16, waiting for transfers between devices, swap(): return lax.ppermute(value, 'rows', [(i, i ^ bit) for i in range(n)])  11.9 us
    pallas_call x1, Pallas kernels, sketch_of(): pl.pallas_call(functools.partial(sketch_kernel, unit, gain, steps, depth)...  6.7 us
    pallas_call x1, Pallas kernels, inverse_of(): pl.pallas_call(inverse_kernel, in_specs=[vmem()], out_specs=vmem(), out_s...  5.45 us
    pallas_call x2, Pallas kernels, cross_of(): pl.pallas_call(functools.partial(cross_kernel, min(512, width), stay), in...  2.86 us
    ppermute x1, waiting for transfers between devices, local(): other = lax.ppermute(part, 'cols', [(i, i ^ step) for i in range(n_cols)])  1.35 us
    dot_general x1, matrix products, local(): lax.dot_general(sketch, inverse, (((1,), (1,)), ((), ())), precision=prec...  1.22 us
  transfers between devices with their start and end apart: 17, of which 9 were waited for; matrix products, arithmetic and copies ran while one was open for 2% of the time, Pallas kernels for 13%

profile of v4, /device:TPU:0, one launch (start us, length us, event | category | flops | bytes accessed | tf_op | source)
XLA Modules:
  0.0 54.7 jit_solution(17728452986180510012)
XLA Ops:
  0.6 6.7 %sketch.1 = (f32[768,4096]{1,0:T(8,128)S(1)}, f32[768,128]{1,0:T(8,128)S(1)}) custom-call(f32[768,4096]{1,0:T(8,128)} %dev_hbm.1, s32[4096,128]{1,0:T(8,128)} %sign_hbm.1), custom_call_target="tpu_custom_call" | custom-call | tf_op jit(solution)/shard_map/sketch/pallas_call | solution.py:71
  7.3 0.5 collective-permute-start
  7.9 1.3 %collective-permute-done.refs_1_ = f32[768,128]{1,0:T(8,128)S(1)} collective-permute-done((f32[768,128]{1,0:T(8,128)S(1)}, f32[768,128]{1,0:T(8,128)S(1)}, u32[]{:S(2)}, u32[]{:S(2)}) %collective-permute-start) | collective-permute-done | bytes 393248 | tf_op jit(solution)/shard_map/ppermute | solution.py:351
  9.2 0.2 join.1
  9.4 1.4 %cross_leave.1 = (f32[128,1024]{1,0:T(8,128)S(1)}, f32[128,1024]{1,0:T(8,128)S(1)}) custom-call(bf16[256,768]{1,0:T(8,128)(2,1)S(1)} %get-tuple-element.34.pair_ref, f32[768,4096]{1,0:T(8,128)S(1)} %get-tuple-element.31.dev_ref), custom_call_target="tpu_custom_call" | custom-call | flops 1000 | bytes 1000 | tf_op jit(solution)/shard_map/cross_leave/pallas_call | solution.py:160
  10.8 2.9 %collective-permute-start.7 = (f32[128,1024]{1,0:T(8,128)S(1)}, f32[128,1024]{1,0:T(8,128)S(1)}, u32[]{:S(2)}, u32[]{:S(2)}) collective-permute-start(f32[128,1024]{1,0:T(8,128)S(1)} %get-tuple-element.32), channel_id=1, source_target_pairs={{0,2},{2,0},{4,6},{6,4},{8,10},{10,8},{12,14},{14,12},{16,18},{18,... | collective-permute-start | bytes 1572872 | tf_op jit(solution)/shard_map/ppermute | solution.py:344
  13.8 1.5 %collective-permute-start.9 = (f32[128,1024]{1,0:T(8,128)S(1)}, f32[128,1024]{1,0:T(8,128)S(1)}, u32[]{:S(2)}, u32[]{:S(2)}) collective-permute-start(f32[128,1024]{1,0:T(8,128)S(1)} %get-tuple-element.33), channel_id=1, source_target_pairs={{0,4},{2,6},{4,0},{6,2},{8,12},{10,14},{12,8},{14,10},{16,20},{18,... | collective-permute-start | bytes 1572872 | tf_op jit(solution)/shard_map/ppermute | solution.py:344
  15.3 0.4 gram.1
  15.6 3.7 %collective-permute-start.3 = (f32[72,128]{1,0:T(8,128)S(1)}, f32[72,128]{1,0:T(8,128)S(1)}, u32[]{:S(2)}, u32[]{:S(2)}) collective-permute-start(f32[72,128]{1,0:T(8,128)S(1)} %gram.1), channel_id=1, source_target_pairs={{0,24},{2,26},{4,28},{6,30},{8,16},{10,18},{12,20},{14,22},{16,8},... | collective-permute-start | bytes 110600 | tf_op jit(solution)/shard_map/ppermute | solution.py:344
  19.3 0.0 collective-permute-start.2
  19.3 0.8 %collective-permute-start.1 = (f32[72,128]{1,0:T(8,128)S(1)}, f32[72,128]{1,0:T(8,128)S(1)}, u32[]{:S(2)}, u32[]{:S(2)}) collective-permute-start(f32[72,128]{1,0:T(8,128)S(1)} %gram.1), channel_id=1, source_target_pairs={{0,8},{2,10},{4,12},{6,14},{8,0},{10,2},{12,4},{14,6},{16,24},{18,... | collective-permute-start | bytes 110600 | tf_op jit(solution)/shard_map/ppermute | solution.py:344
  20.1 1.4 %cross_stay.1 = (f32[128,1024]{1,0:T(8,128)S(1)}, f32[128,1024]{1,0:T(8,128)S(1)}) custom-call(bf16[256,768]{1,0:T(8,128)(2,1)S(1)} %get-tuple-element.34.pair_ref, f32[768,4096]{1,0:T(8,128)S(1)} %get-tuple-element.31.dev_ref), custom_call_target="tpu_custom_call" | custom-call | flops 1000 | bytes 1000 | tf_op jit(solution)/shard_map/cross_stay/pallas_call | solution.py:160
  21.5 0.3 collective-permute-done.3
  21.8 2.3 %collective-permute-done.2 = f32[72,128]{1,0:T(8,128)S(1)} collective-permute-done((f32[72,128]{1,0:T(8,128)S(1)}, f32[72,128]{1,0:T(8,128)S(1)}, u32[]{:S(2)}, u32[]{:S(2)}) %collective-permute-start.2) | collective-permute-done | bytes 36896 | tf_op jit(solution)/shard_map/ppermute | solution.py:344
  24.2 0.0 collective-permute-done.1
  24.2 0.5 %collective-permute-start.6 = (f32[72,128]{1,0:T(8,128)S(1)}, f32[72,128]{1,0:T(8,128)S(1)}, u32[]{:S(2)}, u32[]{:S(2)}) collective-permute-start(f32[72,128]{1,0:T(8,128)S(1)} %add_add_fusion.1), channel_id=1, source_target_pairs={{0,6},{2,4},{4,2},{6,0},{8,14},{10,12},{12,10},{14,8},{16,22},{18,... | collective-permute-start | bytes 110600 | tf_op jit(solution)/shard_map/ppermute | solution.py:344
  24.7 1.5 %collective-permute-start.5 = (f32[72,128]{1,0:T(8,128)S(1)}, f32[72,128]{1,0:T(8,128)S(1)}, u32[]{:S(2)}, u32[]{:S(2)}) collective-permute-start(f32[72,128]{1,0:T(8,128)S(1)} %add_add_fusion.1), channel_id=1, source_target_pairs={{0,4},{2,6},{4,0},{6,2},{8,12},{10,14},{12,8},{14,10},{16,20},{18,... | collective-permute-start | bytes 110600 | tf_op jit(solution)/shard_map/ppermute | solution.py:344
  26.3 1.5 %collective-permute-start.4 = (f32[72,128]{1,0:T(8,128)S(1)}, f32[72,128]{1,0:T(8,128)S(1)}, u32[]{:S(2)}, u32[]{:S(2)}) collective-permute-start(f32[72,128]{1,0:T(8,128)S(1)} %add_add_fusion.1), channel_id=1, source_target_pairs={{0,2},{2,0},{4,6},{6,4},{8,10},{10,8},{12,14},{14,12},{16,18},{18,... | collective-permute-start | bytes 110600 | tf_op jit(solution)/shard_map/ppermute | solution.py:344
  27.7 0.0 collective-permute-done.7.got_ref.got_x
  27.8 0.8 %collective-permute-start.8 = (f32[128,512]{1,0:T(8,128)S(1)}, f32[128,512]{1,0:T(8,128)S(1)}, u32[]{:S(2)}, u32[]{:S(2)}) collective-permute-start(f32[128,512]{1,0:T(8,128)S(1)} %onward.2), channel_id=1, source_target_pairs={{0,4},{2,6},{4,0},{6,2},{8,12},{10,14},{12,8},{14,10},{16,20},{18,... | collective-permute-start | bytes 786440 | tf_op jit(solution)/shard_map/ppermute | solution.py:344
  28.6 0.0 collective-permute-done.9.got_ref.got_y
  28.7 1.6 %collective-permute-start.10 = (f32[128,512]{1,0:T(8,128)S(1)}, f32[128,512]{1,0:T(8,128)S(1)}, u32[]{:S(2)}, u32[]{:S(2)}) collective-permute-start(f32[128,512]{1,0:T(8,128)S(1)} %onward.3), channel_id=1, source_target_pairs={{0,2},{2,0},{4,6},{6,4},{8,10},{10,8},{12,14},{14,12},{16,18},{18,... | collective-permute-start | bytes 786440 | tf_op jit(solution)/shard_map/ppermute | solution.py:344
  30.2 0.0 collective-permute-done.6
  30.2 0.0 collective-permute-done.5
  30.2 0.4 collective-permute-done.4
  30.6 5.4 %inverse.1.inverse_ref = f32[128,128]{1,0:T(8,128)S(1)} custom-call(f32[72,128]{1,0:T(8,128)S(1)} %add_add_fusion.packed_ref), custom_call_target="tpu_custom_call" | custom-call | flops 1000 | bytes 1000 | tf_op jit(solution)/shard_map/inverse/pallas_call | solution.py:225
  36.1 0.0 collective-permute-done.8.then_x
  36.1 0.0 collective-permute-done.10.then_y
  36.1 0.3 project.1
  36.4 2.3 %collective-permute-start.11 = (f32[32,1024]{1,0:T(8,128)S(1)}, f32[32,1024]{1,0:T(8,128)S(1)}, u32[]{:S(2)}, u32[]{:S(2)}) collective-permute-start(f32[32,1024]{1,0:T(8,128)S(1)} %get-tuple-element.40), channel_id=1, source_target_pairs={{0,16},{2,18},{4,20},{6,22},{8,24},{10,26},{12,28},{14,30},{16,0},... | collective-permute-start | bytes 393224 | tf_op jit(solution)/shard_map/ppermute | solution.py:344
  38.7 1.3 %collective-permute-start.12 = (f32[32,1024]{1,0:T(8,128)S(1)}, f32[32,1024]{1,0:T(8,128)S(1)}, u32[]{:S(2)}, u32[]{:S(2)}) collective-permute-start(f32[32,1024]{1,0:T(8,128)S(1)} %get-tuple-element.41), channel_id=1, source_target_pairs={{0,24},{2,26},{4,28},{6,30},{8,16},{10,18},{12,20},{14,22},{16,8},... | collective-permute-start | bytes 393224 | tf_op jit(solution)/shard_map/ppermute | solution.py:344
  40.1 0.2 collective-permute-start.13
  40.3 1.2 %convolution_multiply_fusion = f32[768,128]{1,0:T(8,128)} fusion(f32[768,128]{1,0:T(8,128)S(1)} %get-tuple-element.43, f32[128,128]{1,0:T(8,128)S(1)} %inverse.1.inverse_ref), kind=kOutput, calls=%fused_computation | convolution fusion | flops 151093248 | bytes 851968 | tf_op jit(solution)/shard_map/dot_general | solution.py:372
  41.5 5.9 %collective-permute-done.11.refs_1_ = f32[32,1024]{1,0:T(8,128)S(1)} collective-permute-done((f32[32,1024]{1,0:T(8,128)S(1)}, f32[32,1024]{1,0:T(8,128)S(1)}, u32[]{:S(2)}, u32[]{:S(2)}) %collective-permute-start.11) | collective-permute-done | bytes 131104 | tf_op jit(solution)/shard_map/ppermute | solution.py:344
  47.5 0.0 collective-permute-done.12.refs_2_
  47.5 0.2 collective-permute-done.13.refs_3_
  47.8 1.7 %collective-permute-start.14 = (f32[8,1024]{1,0:T(8,128)S(1)}, f32[8,1024]{1,0:T(8,128)S(1)}, u32[]{:S(2)}, u32[]{:S(2)}) collective-permute-start(f32[8,1024]{1,0:T(8,128)S(1)} %get-tuple-element.50), channel_id=1, source_target_pairs={{0,6},{2,4},{4,2},{6,0},{8,14},{10,12},{12,10},{14,8},{16,22},{18,... | collective-permute-start | bytes 98312 | tf_op jit(solution)/shard_map/ppermute | solution.py:344
  49.5 0.7 %collective-permute-start.15 = (f32[8,1024]{1,0:T(8,128)S(1)}, f32[8,1024]{1,0:T(8,128)S(1)}, u32[]{:S(2)}, u32[]{:S(2)}) collective-permute-start(f32[8,1024]{1,0:T(8,128)S(1)} %get-tuple-element.51), channel_id=1, source_target_pairs={{0,4},{2,6},{4,0},{6,2},{8,12},{10,14},{12,8},{14,10},{16,20},{18,... | collective-permute-start | bytes 98312 | tf_op jit(solution)/shard_map/ppermute | solution.py:344
  50.1 1.2 %collective-permute-start.16 = (f32[8,1024]{1,0:T(8,128)S(1)}, f32[8,1024]{1,0:T(8,128)S(1)}, u32[]{:S(2)}, u32[]{:S(2)}) collective-permute-start(f32[8,1024]{1,0:T(8,128)S(1)} %get-tuple-element.52), channel_id=1, source_target_pairs={{0,2},{2,0},{4,6},{6,4},{8,10},{10,8},{12,14},{14,12},{16,18},{18,... | collective-permute-start | bytes 98312 | tf_op jit(solution)/shard_map/ppermute | solution.py:344
  51.3 1.3 %collective-permute-done.14.refs_3_ = f32[8,1024]{1,0:T(8,128)S(1)} collective-permute-done((f32[8,1024]{1,0:T(8,128)S(1)}, f32[8,1024]{1,0:T(8,128)S(1)}, u32[]{:S(2)}, u32[]{:S(2)}) %collective-permute-start.14) | collective-permute-done | bytes 32800 | tf_op jit(solution)/shard_map/ppermute | solution.py:344
  52.6 0.7 %collective-permute-done.15.refs_2_ = f32[8,1024]{1,0:T(8,128)S(1)} collective-permute-done((f32[8,1024]{1,0:T(8,128)S(1)}, f32[8,1024]{1,0:T(8,128)S(1)}, u32[]{:S(2)}, u32[]{:S(2)}) %collective-permute-start.15) | collective-permute-done | bytes 32800 | tf_op jit(solution)/shard_map/ppermute | solution.py:344
  53.4 0.7 %collective-permute-done.16.refs_1_ = f32[8,1024]{1,0:T(8,128)S(1)} collective-permute-done((f32[8,1024]{1,0:T(8,128)S(1)}, f32[8,1024]{1,0:T(8,128)S(1)}, u32[]{:S(2)}, u32[]{:S(2)}) %collective-permute-start.16) | collective-permute-done | bytes 32800 | tf_op jit(solution)/shard_map/ppermute | solution.py:344
  54.0 0.7 %assemble.1 = f32[8,4096]{1,0:T(8,128)} custom-call(f32[8,1024]{1,0:T(8,128)S(1)} %get-tuple-element.49.refs_0_, f32[8,1024]{1,0:T(8,128)S(1)} %collective-permute-done.16.refs_1_, f32[8,1024]{1,0:T(8,128)S(1)} %collective-permute-done.15.refs_2_, f32[8,1024]{1,0:T(8,128)S(1)} %collective-permute-done.14.refs_3_), custom_call_target="tpu_custom_call" | custom-call | tf_op jit(solution)/shard_map/assemble/pallas_call | solution.py:328
  (5 shorter events, 0.1 us)
Async XLA Ops:
  7.3 1.9 %collective-permute-start = (f32[768,128]{1,0:T(8,128)S(1)}, f32[768,128]{1,0:T(8,128)S(1)}, u32[]{:S(2)}, u32[]{:S(2)}) collective-permute-start(f32[768,128]{1,0:T(8,128)S(1)} %get-tuple-element.29.refs_0_), channel_id=1, source_target_pairs={{0,1},{1,0},{2,3},{3,2},{4,5},{5,4},{6,7},{7,6},{8,9},{9,8},{10,11... | collective-permute-start | bytes 1179656 | tf_op jit(solution)/shard_map/ppermute | solution.py:351
  10.8 16.9 %collective-permute-start.7 = (f32[128,1024]{1,0:T(8,128)S(1)}, f32[128,1024]{1,0:T(8,128)S(1)}, u32[]{:S(2)}, u32[]{:S(2)}) collective-permute-start(f32[128,1024]{1,0:T(8,128)S(1)} %get-tuple-element.32), channel_id=1, source_target_pairs={{0,2},{2,0},{4,6},{6,4},{8,10},{10,8},{12,14},{14,12},{16,18},{18,... | collective-permute-start | bytes 1572872 | tf_op jit(solution)/shard_map/ppermute | solution.py:344
  13.8 14.9 %collective-permute-start.9 = (f32[128,1024]{1,0:T(8,128)S(1)}, f32[128,1024]{1,0:T(8,128)S(1)}, u32[]{:S(2)}, u32[]{:S(2)}) collective-permute-start(f32[128,1024]{1,0:T(8,128)S(1)} %get-tuple-element.33), channel_id=1, source_target_pairs={{0,4},{2,6},{4,0},{6,2},{8,12},{10,14},{12,8},{14,10},{16,20},{18,... | collective-permute-start | bytes 1572872 | tf_op jit(solution)/shard_map/ppermute | solution.py:344
  15.6 6.2 %collective-permute-start.3 = (f32[72,128]{1,0:T(8,128)S(1)}, f32[72,128]{1,0:T(8,128)S(1)}, u32[]{:S(2)}, u32[]{:S(2)}) collective-permute-start(f32[72,128]{1,0:T(8,128)S(1)} %gram.1), channel_id=1, source_target_pairs={{0,24},{2,26},{4,28},{6,30},{8,16},{10,18},{12,20},{14,22},{16,8},... | collective-permute-start | bytes 110600 | tf_op jit(solution)/shard_map/ppermute | solution.py:344
  19.3 4.9 %collective-permute-start.2 = (f32[72,128]{1,0:T(8,128)S(1)}, f32[72,128]{1,0:T(8,128)S(1)}, u32[]{:S(2)}, u32[]{:S(2)}) collective-permute-start(f32[72,128]{1,0:T(8,128)S(1)} %gram.1), channel_id=1, source_target_pairs={{0,16},{2,18},{4,20},{6,22},{8,24},{10,26},{12,28},{14,30},{16,0},... | collective-permute-start | bytes 110600 | tf_op jit(solution)/shard_map/ppermute | solution.py:344
  19.3 4.9 %collective-permute-start.1 = (f32[72,128]{1,0:T(8,128)S(1)}, f32[72,128]{1,0:T(8,128)S(1)}, u32[]{:S(2)}, u32[]{:S(2)}) collective-permute-start(f32[72,128]{1,0:T(8,128)S(1)} %gram.1), channel_id=1, source_target_pairs={{0,8},{2,10},{4,12},{6,14},{8,0},{10,2},{12,4},{14,6},{16,24},{18,... | collective-permute-start | bytes 110600 | tf_op jit(solution)/shard_map/ppermute | solution.py:344
  24.2 6.0 %collective-permute-start.6 = (f32[72,128]{1,0:T(8,128)S(1)}, f32[72,128]{1,0:T(8,128)S(1)}, u32[]{:S(2)}, u32[]{:S(2)}) collective-permute-start(f32[72,128]{1,0:T(8,128)S(1)} %add_add_fusion.1), channel_id=1, source_target_pairs={{0,6},{2,4},{4,2},{6,0},{8,14},{10,12},{12,10},{14,8},{16,22},{18,... | collective-permute-start | bytes 110600 | tf_op jit(solution)/shard_map/ppermute | solution.py:344
  24.7 5.5 %collective-permute-start.5 = (f32[72,128]{1,0:T(8,128)S(1)}, f32[72,128]{1,0:T(8,128)S(1)}, u32[]{:S(2)}, u32[]{:S(2)}) collective-permute-start(f32[72,128]{1,0:T(8,128)S(1)} %add_add_fusion.1), channel_id=1, source_target_pairs={{0,4},{2,6},{4,0},{6,2},{8,12},{10,14},{12,8},{14,10},{16,20},{18,... | collective-permute-start | bytes 110600 | tf_op jit(solution)/shard_map/ppermute | solution.py:344
  26.3 4.4 %collective-permute-start.4 = (f32[72,128]{1,0:T(8,128)S(1)}, f32[72,128]{1,0:T(8,128)S(1)}, u32[]{:S(2)}, u32[]{:S(2)}) collective-permute-start(f32[72,128]{1,0:T(8,128)S(1)} %add_add_fusion.1), channel_id=1, source_target_pairs={{0,2},{2,0},{4,6},{6,4},{8,10},{10,8},{12,14},{14,12},{16,18},{18,... | collective-permute-start | bytes 110600 | tf_op jit(solution)/shard_map/ppermute | solution.py:344
  27.8 8.3 %collective-permute-start.8 = (f32[128,512]{1,0:T(8,128)S(1)}, f32[128,512]{1,0:T(8,128)S(1)}, u32[]{:S(2)}, u32[]{:S(2)}) collective-permute-start(f32[128,512]{1,0:T(8,128)S(1)} %onward.2), channel_id=1, source_target_pairs={{0,4},{2,6},{4,0},{6,2},{8,12},{10,14},{12,8},{14,10},{16,20},{18,... | collective-permute-start | bytes 786440 | tf_op jit(solution)/shard_map/ppermute | solution.py:344
  28.7 7.4 %collective-permute-start.10 = (f32[128,512]{1,0:T(8,128)S(1)}, f32[128,512]{1,0:T(8,128)S(1)}, u32[]{:S(2)}, u32[]{:S(2)}) collective-permute-start(f32[128,512]{1,0:T(8,128)S(1)} %onward.3), channel_id=1, source_target_pairs={{0,2},{2,0},{4,6},{6,4},{8,10},{10,8},{12,14},{14,12},{16,18},{18,... | collective-permute-start | bytes 786440 | tf_op jit(solution)/shard_map/ppermute | solution.py:344
  36.4 11.0 %collective-permute-start.11 = (f32[32,1024]{1,0:T(8,128)S(1)}, f32[32,1024]{1,0:T(8,128)S(1)}, u32[]{:S(2)}, u32[]{:S(2)}) collective-permute-start(f32[32,1024]{1,0:T(8,128)S(1)} %get-tuple-element.40), channel_id=1, source_target_pairs={{0,16},{2,18},{4,20},{6,22},{8,24},{10,26},{12,28},{14,30},{16,0},... | collective-permute-start | bytes 393224 | tf_op jit(solution)/shard_map/ppermute | solution.py:344
  38.7 8.7 %collective-permute-start.12 = (f32[32,1024]{1,0:T(8,128)S(1)}, f32[32,1024]{1,0:T(8,128)S(1)}, u32[]{:S(2)}, u32[]{:S(2)}) collective-permute-start(f32[32,1024]{1,0:T(8,128)S(1)} %get-tuple-element.41), channel_id=1, source_target_pairs={{0,24},{2,26},{4,28},{6,30},{8,16},{10,18},{12,20},{14,22},{16,8},... | collective-permute-start | bytes 393224 | tf_op jit(solution)/shard_map/ppermute | solution.py:344
  40.1 7.6 %collective-permute-start.13 = (f32[32,1024]{1,0:T(8,128)S(1)}, f32[32,1024]{1,0:T(8,128)S(1)}, u32[]{:S(2)}, u32[]{:S(2)}) collective-permute-start(f32[32,1024]{1,0:T(8,128)S(1)} %get-tuple-element.42), channel_id=1, source_target_pairs={{0,8},{2,10},{4,12},{6,14},{8,0},{10,2},{12,4},{14,6},{16,24},{18,... | collective-permute-start | bytes 393224 | tf_op jit(solution)/shard_map/ppermute | solution.py:344
  47.8 4.9 %collective-permute-start.14 = (f32[8,1024]{1,0:T(8,128)S(1)}, f32[8,1024]{1,0:T(8,128)S(1)}, u32[]{:S(2)}, u32[]{:S(2)}) collective-permute-start(f32[8,1024]{1,0:T(8,128)S(1)} %get-tuple-element.50), channel_id=1, source_target_pairs={{0,6},{2,4},{4,2},{6,0},{8,14},{10,12},{12,10},{14,8},{16,22},{18,... | collective-permute-start | bytes 98312 | tf_op jit(solution)/shard_map/ppermute | solution.py:344
  49.5 3.9 %collective-permute-start.15 = (f32[8,1024]{1,0:T(8,128)S(1)}, f32[8,1024]{1,0:T(8,128)S(1)}, u32[]{:S(2)}, u32[]{:S(2)}) collective-permute-start(f32[8,1024]{1,0:T(8,128)S(1)} %get-tuple-element.51), channel_id=1, source_target_pairs={{0,4},{2,6},{4,0},{6,2},{8,12},{10,14},{12,8},{14,10},{16,20},{18,... | collective-permute-start | bytes 98312 | tf_op jit(solution)/shard_map/ppermute | solution.py:344
  50.1 3.9 %collective-permute-start.16 = (f32[8,1024]{1,0:T(8,128)S(1)}, f32[8,1024]{1,0:T(8,128)S(1)}, u32[]{:S(2)}, u32[]{:S(2)}) collective-permute-start(f32[8,1024]{1,0:T(8,128)S(1)} %get-tuple-element.52), channel_id=1, source_target_pairs={{0,2},{2,0},{4,6},{6,4},{8,10},{10,8},{12,14},{14,12},{16,18},{18,... | collective-permute-start | bytes 98312 | tf_op jit(solution)/shard_map/ppermute | solution.py:344

commit v5 on v4

--- a/solution.py
+++ b/solution.py
@@ -38,50 +38,72 @@
     return pltpu.CompilerParams(vmem_limit_bytes=mib * MIB)
 
 
-def sketch_kernel(unit, gain, steps, depth, dev_hbm, sign_hbm, dev_ref, out_ref, sign_buf, omega, dev_sem, sign_sem):
-    block = dev_ref.shape[0] // steps
+PARTS, DEPTH = (3, 3, 2, 4), 3
+
+
+def sketch_kernel(unit, gain, dev_hbm, sign_hbm, dev_ref, omega, out_ref, sign_buf, dev_sem, sign_sem):
+    unit_rows = dev_ref.shape[0] // sum(PARTS)
+    bounds = [sum(PARTS[:i]) * unit_rows for i in range(len(PARTS) + 1)]
     signs = pltpu.make_async_copy(sign_hbm, sign_buf, sign_sem)
     signs.start()
 
     def fetch(i):
-        here = pl.ds(i * block, block)
+        here = pl.ds(bounds[i], bounds[i + 1] - bounds[i])
         return pltpu.make_async_copy(dev_hbm.at[here, :], dev_ref.at[here, :], dev_sem.at[i])
 
-    for i in range(depth - 1):
+    for i in range(DEPTH - 1):
         fetch(i).start()
     signs.wait()
     omega[...] = (sign_buf[...].astype(jnp.float32) * unit).astype(jnp.bfloat16)
-    for i in range(steps):
-        if i + depth - 1 < steps:
-            fetch(i + depth - 1).start()
+    for i in range(len(PARTS)):
+        if i + DEPTH - 1 < len(PARTS):
+            fetch(i + DEPTH - 1).start()
         fetch(i).wait()
-        here = slice(i * block, (i + 1) * block)
-        high, low = split(dev_ref[here, :])
-        out_ref[here, :] = (dot(high, omega[...]) + dot(low, omega[...])) * gain
+        if i < len(PARTS) - 1:
+            here = slice(bounds[i], bounds[i + 1])
+            high, low = split(dev_ref[here, :])
+            out_ref[here, :] = (dot(high, omega[...]) + dot(low, omega[...])) * gain
+
+
+def last_sketch_kernel(gain, dev_ref, omega, out_ref):
+    high, low = split(dev_ref[dev_ref.shape[0] - out_ref.shape[0]:, :])
+    out_ref[...] = (dot(high, omega[...]) + dot(low, omega[...])) * gain
 
 
 def sketch_of(dev, signs):
     rows, cols = dev.shape
     rank = signs.shape[1]
-    steps, depth = 4, 3
+    block = rows // sum(PARTS) * PARTS[-1]
     unit = 2.0 ** -math.ceil(math.log2(math.sqrt(SCANS)))
     gain = 1.0 / (math.sqrt(SCANS) * unit)
     dev = pltpu.with_memory_space_constraint(dev, pltpu.HBM)
     signs = pltpu.with_memory_space_constraint(signs, pltpu.HBM)
-    return pl.pallas_call(
-        functools.partial(sketch_kernel, unit, gain, steps, depth),
+    kept, omega, most = pl.pallas_call(
+        functools.partial(sketch_kernel, unit, gain),
         in_specs=[pl.BlockSpec(memory_space=pltpu.HBM)] * 2,
-        out_specs=[vmem()] * 2,
-        out_shape=[pltpu.VMEM((rows, cols), jnp.float32), pltpu.VMEM((rows, rank), jnp.float32)],
+        out_specs=[vmem()] * 3,
+        out_shape=[
+            pltpu.VMEM((rows, cols), jnp.float32),
+            pltpu.VMEM((cols, rank), jnp.bfloat16),
+            pltpu.VMEM((rows - block, rank), jnp.float32),
+        ],
         scratch_shapes=[
             pltpu.VMEM((cols, rank), jnp.int32),
-            pltpu.VMEM((cols, rank), jnp.bfloat16),
-            pltpu.SemaphoreType.DMA((steps,)),
+            pltpu.SemaphoreType.DMA((len(PARTS),)),
             pltpu.SemaphoreType.DMA,
         ],
         compiler_params=params(24),
         name="sketch",
     )(dev, signs)
+    last = pl.pallas_call(
+        functools.partial(last_sketch_kernel, gain),
+        in_specs=[vmem()] * 2,
+        out_specs=vmem(),
+        out_shape=jax.ShapeDtypeStruct((block, rank), jnp.float32),
+        compiler_params=params(8),
+        name="last_sketch",
+    )(kept, omega)
+    return kept, most, last
 
 
 def join_kernel(parts, *refs):
@@ -115,9 +137,12 @@
     return lax.broadcasted_iota(jnp.int32, shape, 0), lax.broadcasted_iota(jnp.int32, shape, 1)
 
 
-def gram_kernel(pair_ref, packed_ref):
-    four = lax.dot_general(
-        pair_ref[...], pair_ref[...], (((1,), (1,)), ((), ())), preferred_element_type=jnp.float32
+def gram_kernel(most_ref, last_ref, packed_ref):
+    four = sum(
+        lax.dot_general(
+            ref[...], ref[...], (((1,), (1,)), ((), ())), preferred_element_type=jnp.float32
+        )
+        for ref in (most_ref, last_ref)
     )
     rank = four.shape[0] // 2
     gram = (four[:rank, :rank] + four[rank:, rank:]) + (four[:rank, rank:] + four[rank:, :rank])
@@ -129,43 +154,50 @@
     packed_ref[half:, :] = jnp.broadcast_to(diagonal, (8, last.shape[1]))
 
 
-def gram_of(pair):
+def gram_of(pair, last):
     rank = pair.shape[0] // 2
     return pl.pallas_call(
         gram_kernel,
-        in_specs=[vmem()],
+        in_specs=[vmem()] * 2,
         out_specs=vmem(),
         out_shape=jax.ShapeDtypeStruct((rank // 2 + 8, rank), jnp.float32),
         compiler_params=params(8),
         cost_estimate=little,
         name="gram",
-    )(pair)
-
-
-def cross_kernel(block, stay, pair_ref, dev_ref, *outs):
+    )(pair, last)
+
+
+def cross_kernel(block, stay, starts, *refs):
+    pairs, dev_ref, prior, outs = refs[:len(starts)], refs[len(starts)], refs[len(starts) + 1:-2], refs[-2:]
     rank, width = outs[0].shape
     x, y = place()[:2]
     chunks = (x, 2 + y) if stay else (1 - x, 3 - y)
-    for chunk, out in zip(chunks, outs):
+    for j, (chunk, out) in enumerate(zip(chunks, outs)):
         for t in range(width // block):
             start = pl.multiple_of(chunk * width + t * block, 128)
-            high, low = split(dev_ref[:, pl.ds(start, block)])
-            both = dot(pair_ref[...], high)
-            out[:, t * block:(t + 1) * block] = (both[:rank] + both[rank:]) + dot(pair_ref[:rank, :], low)
-
-
-def cross_of(stay, pair, dev):
-    rank, rows = pair.shape[0] // 2, pair.shape[1]
+            here = slice(t * block, (t + 1) * block)
+            value = prior[j][:, here] if prior else None
+            for first, pair in zip(starts, pairs):
+                high, low = split(dev_ref[first:first + pair.shape[1], pl.ds(start, block)])
+                both = dot(pair[...], high)
+                term = (both[:rank] + both[rank:]) + dot(pair[:rank, :], low)
+                value = term if value is None else value + term
+            out[:, here] = value
+
+
+def cross_of(stay, pairs, dev, prior=()):
+    starts, pairs = list(pairs), list(pairs.values())
+    rank = pairs[0].shape[0] // 2
     width = dev.shape[1] // 4
     return pl.pallas_call(
-        functools.partial(cross_kernel, min(512, width), stay),
-        in_specs=[vmem()] * 2,
+        functools.partial(cross_kernel, min(512, width), stay, starts),
+        in_specs=[vmem()] * (len(pairs) + 1 + len(prior)),
         out_specs=[vmem()] * 2,
         out_shape=[jax.ShapeDtypeStruct((rank, width), jnp.float32)] * 2,
         compiler_params=params(8),
         cost_estimate=little,
         name="cross_stay" if stay else "cross_leave",
-    )(pair, dev)
+    )(*pairs, dev, *prior)
 
 
 def thirds(value):
@@ -343,18 +375,25 @@
     def swap(value, bit):
         return lax.ppermute(value, "rows", [(i, i ^ bit) for i in range(n)])
 
-    kept, part = sketch_of(deviations, test_signs)
-    step = 1
-    while 2 * step < n_cols:
-        part = part + lax.ppermute(part, "cols", [(i, i ^ step) for i in range(n_cols)])
-        step *= 2
-    other = lax.ppermute(part, "cols", [(i, i ^ step) for i in range(n_cols)])
-    sketch, pair = join(part, other)
-
-    leave = cross_of(False, pair, kept)
-    stay = cross_of(True, pair, kept)
-
-    gram = gram_of(lax.optimization_barrier((pair, leave))[0])
+    def over_cols(part):
+        step = 1
+        while 2 * step < n_cols:
+            part = part + lax.ppermute(part, "cols", [(i, i ^ step) for i in range(n_cols)])
+            step *= 2
+        return part, lax.ppermute(part, "cols", [(i, i ^ step) for i in range(n_cols)])
+
+    kept, most, last = sketch_of(deviations, test_signs)
+    sketch, pair = join(*over_cols(most))
+    last = over_cols(last)
+    tail = rows - last[0].shape[0]
+
+    leave = cross_of(False, {0: pair}, kept)
+    last, leave = lax.optimization_barrier((last, leave))
+    last_sketch, last_pair = join(*last)
+    leave = cross_of(False, {tail: last_pair}, kept, leave)
+    stay = cross_of(True, {0: pair, tail: last_pair}, kept)
+
+    gram = gram_of(*lax.optimization_barrier((pair, last_pair, leave))[:2])
     steps, beside = [4 ** i for i in range(1, n) if 4 ** i < n] + [1], [stay]
     for step in steps:
         found = [swap(gram, step * k) for k in range(1, min(4, n // step))]
@@ -370,7 +409,7 @@
 
     groups = project(n, inverse, stay[0], got_x, then_x, stay[1], got_y, then_y)
     basis = lax.dot_general(
-        sketch, inverse, (((1,), (1,)), ((), ())),
+        jnp.concatenate([sketch, last_sketch]), inverse, (((1,), (1,)), ((), ())),
         precision=precise, preferred_element_type=jnp.float32,
     ) * math.sqrt(samples)
     order = sorted(range(1, n // 4), key=lambda k: (k == 1, k))

time: 54.8 us -> 54.3 us (level)
  waiting for transfers between devices: 13.3 us -> 12.1 us
    ppermute x1 -> x2, waiting for transfers between devices: 1.35 us -> 0.14 us  [over_cols(): lax.ppermute(part, 'cols', [(i, i ^ step) for i in range(n_cols)])]
    pallas_call x4 -> x6, Pallas kernels: 9.94 us -> 10.3 us  [the longest x1 5.58 us: sketch_of(): pl.pallas_call(functools.partial(sketch_kernel, unit, gain), in_specs=[pl...]
  transfers between devices with their start and end apart: 17 -> 18, of which waited for: 9 -> 9; matrix products, arithmetic and copies ran while one was open for 2% -> 2% of each run, Pallas kernels for 13% -> 18%
where the time goes in v5:
time: 54.3 us; the launch traced here: 54.1 us
  starting transfers between devices  22.9 us (42%)
  Pallas kernels  17.1 us (31%)
  waiting for transfers between devices  12.1 us (22%)
  matrix products  1.22 us (2%)
  between operations  0.73 us (1%)
    ppermute x16, starting transfers between devices, swap(): return lax.ppermute(value, 'rows', [(i, i ^ bit) for i in range(n)])  22.2 us
    ppermute x16, waiting for transfers between devices, swap(): return lax.ppermute(value, 'rows', [(i, i ^ bit) for i in range(n)])  12 us
    pallas_call x1, Pallas kernels, sketch_of(): pl.pallas_call(functools.partial(sketch_kernel, unit, gain), in_specs=[pl...  5.58 us
    pallas_call x1, Pallas kernels, inverse_of(): pl.pallas_call(inverse_kernel, in_specs=[vmem()], out_specs=vmem(), out_s...  5.45 us
    pallas_call x3, Pallas kernels, cross_of(): pl.pallas_call(functools.partial(cross_kernel, min(512, width), stay, sta...  3.12 us
    pallas_call x1, Pallas kernels, sketch_of(): pl.pallas_call(functools.partial(last_sketch_kernel, gain), in_specs=[vme...  1.25 us
    dot_general x1, matrix products, local(): lax.dot_general(jnp.concatenate([sketch, last_sketch]), inverse, (((1,),...  1.22 us
  transfers between devices with their start and end apart: 18, of which 9 were waited for; matrix products, arithmetic and copies ran while one was open for 2% of the time, Pallas kernels for 18%

profile of v5, /device:TPU:0, one launch (start us, length us, event | category | flops | bytes accessed | tf_op | source)
XLA Modules:
  0.0 54.1 jit_solution(6586250877997753741)
XLA Ops:
  0.6 5.6 %sketch.1 = (f32[768,4096]{1,0:T(8,128)S(1)}, bf16[4096,128]{1,0:T(8,128)(2,1)S(1)}, f32[512,128]{1,0:T(8,128)S(1)}) custom-call(f32[768,4096]{1,0:T(8,128)} %dev_hbm.1, s32[4096,128]{1,0:T(8,128)} %sign_hbm.1), custom_call_target="tpu_custom_call" | custom-call | tf_op jit(solution)/shard_map/sketch/pallas_call | solution.py:81
  6.2 0.5 collective-permute-start
  6.7 1.3 %last_sketch.1.refs_0_ = f32[256,128]{1,0:T(8,128)S(1)} custom-call(f32[768,4096]{1,0:T(8,128)S(1)} %get-tuple-element.41.dev_ref.refs_1_.refs_2_, bf16[4096,128]{1,0:T(8,128)(2,1)S(1)} %get-tuple-element.42.omega), custom_call_target="tpu_custom_call" | custom-call | tf_op jit(solution)/shard_map/last_sketch/pallas_call | solution.py:98
  8.0 0.1 collective-permute-start.1
  8.1 0.0 collective-permute-done.refs_1_
  8.1 0.1 join.2
  8.3 1.0 %cross_leave.2 = (f32[128,1024]{1,0:T(8,128)S(1)}, f32[128,1024]{1,0:T(8,128)S(1)}) custom-call(bf16[256,512]{1,0:T(8,128)(2,1)S(1)} %get-tuple-element.52.refs_0_.most_ref, f32[768,4096]{1,0:T(8,128)S(1)} %get-tuple-element.41.dev_ref.refs_1_.refs_2_), custom_call_target="tpu_custom_call" | custom-call | flops 1000 | bytes 1000 | tf_op jit(solution)/shard_map/cross_leave/pallas_call | solution.py:192
  9.3 0.1 collective-permute-done.1.refs_1_
  9.4 0.1 join.3
  9.5 0.6 %cross_leave.3 = (f32[128,1024]{1,0:T(8,128)S(1)}, f32[128,1024]{1,0:T(8,128)S(1)}) custom-call(bf16[256,256]{1,0:T(8,128)(2,1)S(1)} %get-tuple-element.53.refs_0_.last_ref.refs_1_, f32[768,4096]{1,0:T(8,128)S(1)} %get-tuple-element.41.dev_ref.refs_1_.refs_2_, f32[128,1024]{1,0:T(8,128)S(1)} %get-tuple-element.48.refs_2_, ...), custom_call_target="tpu_custom_call" | custom-call | flops 1000 | bytes 1000 | tf_op jit(solution)/shard_map/cross_leave/pallas_call | solution.py:192
  10.1 2.9 %collective-permute-start.8 = (f32[128,1024]{1,0:T(8,128)S(1)}, f32[128,1024]{1,0:T(8,128)S(1)}, u32[]{:S(2)}, u32[]{:S(2)}) collective-permute-start(f32[128,1024]{1,0:T(8,128)S(1)} %get-tuple-element.50), channel_id=1, source_target_pairs={{0,2},{2,0},{4,6},{6,4},{8,10},{10,8},{12,14},{14,12},{16,18},{18,... | collective-permute-start | bytes 1572872 | tf_op jit(solution)/shard_map/ppermute | solution.py:376
  13.0 1.5 %collective-permute-start.10 = (f32[128,1024]{1,0:T(8,128)S(1)}, f32[128,1024]{1,0:T(8,128)S(1)}, u32[]{:S(2)}, u32[]{:S(2)}) collective-permute-start(f32[128,1024]{1,0:T(8,128)S(1)} %get-tuple-element.51), channel_id=1, source_target_pairs={{0,4},{2,6},{4,0},{6,2},{8,12},{10,14},{12,8},{14,10},{16,20},{18,... | collective-permute-start | bytes 1572872 | tf_op jit(solution)/shard_map/ppermute | solution.py:376
  14.5 0.4 gram.1
  14.9 3.7 %collective-permute-start.4 = (f32[72,128]{1,0:T(8,128)S(1)}, f32[72,128]{1,0:T(8,128)S(1)}, u32[]{:S(2)}, u32[]{:S(2)}) collective-permute-start(f32[72,128]{1,0:T(8,128)S(1)} %gram.1), channel_id=1, source_target_pairs={{0,24},{2,26},{4,28},{6,30},{8,16},{10,18},{12,20},{14,22},{16,8},... | collective-permute-start | bytes 110600 | tf_op jit(solution)/shard_map/ppermute | solution.py:376
  18.6 0.0 collective-permute-start.3
  18.6 0.8 %collective-permute-start.2 = (f32[72,128]{1,0:T(8,128)S(1)}, f32[72,128]{1,0:T(8,128)S(1)}, u32[]{:S(2)}, u32[]{:S(2)}) collective-permute-start(f32[72,128]{1,0:T(8,128)S(1)} %gram.1), channel_id=1, source_target_pairs={{0,8},{2,10},{4,12},{6,14},{8,0},{10,2},{12,4},{14,6},{16,24},{18,... | collective-permute-start | bytes 110600 | tf_op jit(solution)/shard_map/ppermute | solution.py:376
  19.4 1.5 %cross_stay.1 = (f32[128,1024]{1,0:T(8,128)S(1)}, f32[128,1024]{1,0:T(8,128)S(1)}) custom-call(bf16[256,512]{1,0:T(8,128)(2,1)S(1)} %get-tuple-element.52.refs_0_.most_ref, bf16[256,256]{1,0:T(8,128)(2,1)S(1)} %get-tuple-element.53.refs_0_.last_ref.refs_1_, f32[768,4096]{1,0:T(8,128)S(1)} %get-tuple-element.41.dev_ref.refs_1_.refs_2_), custom_call_target="tpu_custom_call" | custom-call | flops 1000 | bytes 1000 | tf_op jit(solution)/shard_map/cross_stay/pallas_call | solution.py:192
  20.9 0.2 collective-permute-done.4
  21.1 2.4 %collective-permute-done.3 = f32[72,128]{1,0:T(8,128)S(1)} collective-permute-done((f32[72,128]{1,0:T(8,128)S(1)}, f32[72,128]{1,0:T(8,128)S(1)}, u32[]{:S(2)}, u32[]{:S(2)}) %collective-permute-start.3) | collective-permute-done | bytes 36896 | tf_op jit(solution)/shard_map/ppermute | solution.py:376
  23.5 0.0 collective-permute-done.2
  23.5 0.5 collective-permute-start.7
  24.0 1.5 %collective-permute-start.6 = (f32[72,128]{1,0:T(8,128)S(1)}, f32[72,128]{1,0:T(8,128)S(1)}, u32[]{:S(2)}, u32[]{:S(2)}) collective-permute-start(f32[72,128]{1,0:T(8,128)S(1)} %add_add_fusion.1), channel_id=1, source_target_pairs={{0,4},{2,6},{4,0},{6,2},{8,12},{10,14},{12,8},{14,10},{16,20},{18,... | collective-permute-start | bytes 110600 | tf_op jit(solution)/shard_map/ppermute | solution.py:376
  25.5 1.5 %collective-permute-start.5 = (f32[72,128]{1,0:T(8,128)S(1)}, f32[72,128]{1,0:T(8,128)S(1)}, u32[]{:S(2)}, u32[]{:S(2)}) collective-permute-start(f32[72,128]{1,0:T(8,128)S(1)} %add_add_fusion.1), channel_id=1, source_target_pairs={{0,2},{2,0},{4,6},{6,4},{8,10},{10,8},{12,14},{14,12},{16,18},{18,... | collective-permute-start | bytes 110600 | tf_op jit(solution)/shard_map/ppermute | solution.py:376
  27.0 0.0 collective-permute-done.8.got_ref.got_x
  27.1 0.8 %collective-permute-start.9 = (f32[128,512]{1,0:T(8,128)S(1)}, f32[128,512]{1,0:T(8,128)S(1)}, u32[]{:S(2)}, u32[]{:S(2)}) collective-permute-start(f32[128,512]{1,0:T(8,128)S(1)} %onward.2), channel_id=1, source_target_pairs={{0,4},{2,6},{4,0},{6,2},{8,12},{10,14},{12,8},{14,10},{16,20},{18,... | collective-permute-start | bytes 786440 | tf_op jit(solution)/shard_map/ppermute | solution.py:376
  27.9 0.0 collective-permute-done.10.got_ref.got_y
  28.0 1.6 %collective-permute-start.11 = (f32[128,512]{1,0:T(8,128)S(1)}, f32[128,512]{1,0:T(8,128)S(1)}, u32[]{:S(2)}, u32[]{:S(2)}) collective-permute-start(f32[128,512]{1,0:T(8,128)S(1)} %onward.3), channel_id=1, source_target_pairs={{0,2},{2,0},{4,6},{6,4},{8,10},{10,8},{12,14},{14,12},{16,18},{18,... | collective-permute-start | bytes 786440 | tf_op jit(solution)/shard_map/ppermute | solution.py:376
  29.5 0.0 collective-permute-done.7
  29.5 0.0 collective-permute-done.6
  29.5 0.4 collective-permute-done.5
  29.9 5.5 %inverse.1.inverse_ref = f32[128,128]{1,0:T(8,128)S(1)} custom-call(f32[72,128]{1,0:T(8,128)S(1)} %add_add_fusion.packed_ref), custom_call_target="tpu_custom_call" | custom-call | flops 1000 | bytes 1000 | tf_op jit(solution)/shard_map/inverse/pallas_call | solution.py:257
  35.3 0.0 collective-permute-done.9.then_x
  35.4 0.0 collective-permute-done.11.then_y
  35.4 0.3 project.1
  35.7 2.3 %collective-permute-start.12 = (f32[32,1024]{1,0:T(8,128)S(1)}, f32[32,1024]{1,0:T(8,128)S(1)}, u32[]{:S(2)}, u32[]{:S(2)}) collective-permute-start(f32[32,1024]{1,0:T(8,128)S(1)} %get-tuple-element.59), channel_id=1, source_target_pairs={{0,16},{2,18},{4,20},{6,22},{8,24},{10,26},{12,28},{14,30},{16,0},... | collective-permute-start | bytes 393224 | tf_op jit(solution)/shard_map/ppermute | solution.py:376
  38.0 1.3 %collective-permute-start.13 = (f32[32,1024]{1,0:T(8,128)S(1)}, f32[32,1024]{1,0:T(8,128)S(1)}, u32[]{:S(2)}, u32[]{:S(2)}) collective-permute-start(f32[32,1024]{1,0:T(8,128)S(1)} %get-tuple-element.60), channel_id=1, source_target_pairs={{0,24},{2,26},{4,28},{6,30},{8,16},{10,18},{12,20},{14,22},{16,8},... | collective-permute-start | bytes 393224 | tf_op jit(solution)/shard_map/ppermute | solution.py:376
  39.4 0.2 collective-permute-start.14
  39.6 1.2 %convolution_multiply_fusion = f32[768,128]{1,0:T(8,128)} fusion(f32[128,128]{1,0:T(8,128)S(1)} %inverse.1.inverse_ref, f32[256,128]{1,0:T(8,128)S(1)} %get-tuple-element.63, f32[512,128]{1,0:T(8,128)S(1)} %get-tuple-element.62), kind=kOutput, calls=%fused_computation | convolution fusion | flops 151191552 | bytes 851968 | tf_op jit(solution)/shard_map/dot_general | solution.py:411
  40.8 6.0 %collective-permute-done.12.refs_1_ = f32[32,1024]{1,0:T(8,128)S(1)} collective-permute-done((f32[32,1024]{1,0:T(8,128)S(1)}, f32[32,1024]{1,0:T(8,128)S(1)}, u32[]{:S(2)}, u32[]{:S(2)}) %collective-permute-start.12) | collective-permute-done | bytes 131104 | tf_op jit(solution)/shard_map/ppermute | solution.py:376
  46.9 0.0 collective-permute-done.13.refs_2_
  46.9 0.2 collective-permute-done.14.refs_3_
  47.1 1.7 %collective-permute-start.15 = (f32[8,1024]{1,0:T(8,128)S(1)}, f32[8,1024]{1,0:T(8,128)S(1)}, u32[]{:S(2)}, u32[]{:S(2)}) collective-permute-start(f32[8,1024]{1,0:T(8,128)S(1)} %get-tuple-element.70), channel_id=1, source_target_pairs={{0,6},{2,4},{4,2},{6,0},{8,14},{10,12},{12,10},{14,8},{16,22},{18,... | collective-permute-start | bytes 98312 | tf_op jit(solution)/shard_map/ppermute | solution.py:376
  48.8 0.8 %collective-permute-start.16 = (f32[8,1024]{1,0:T(8,128)S(1)}, f32[8,1024]{1,0:T(8,128)S(1)}, u32[]{:S(2)}, u32[]{:S(2)}) collective-permute-start(f32[8,1024]{1,0:T(8,128)S(1)} %get-tuple-element.71), channel_id=1, source_target_pairs={{0,4},{2,6},{4,0},{6,2},{8,12},{10,14},{12,8},{14,10},{16,20},{18,... | collective-permute-start | bytes 98312 | tf_op jit(solution)/shard_map/ppermute | solution.py:376
  49.5 1.1 %collective-permute-start.17 = (f32[8,1024]{1,0:T(8,128)S(1)}, f32[8,1024]{1,0:T(8,128)S(1)}, u32[]{:S(2)}, u32[]{:S(2)}) collective-permute-start(f32[8,1024]{1,0:T(8,128)S(1)} %get-tuple-element.72), channel_id=1, source_target_pairs={{0,2},{2,0},{4,6},{6,4},{8,10},{10,8},{12,14},{14,12},{16,18},{18,... | collective-permute-start | bytes 98312 | tf_op jit(solution)/shard_map/ppermute | solution.py:376
  50.6 1.3 %collective-permute-done.15.refs_3_ = f32[8,1024]{1,0:T(8,128)S(1)} collective-permute-done((f32[8,1024]{1,0:T(8,128)S(1)}, f32[8,1024]{1,0:T(8,128)S(1)}, u32[]{:S(2)}, u32[]{:S(2)}) %collective-permute-start.15) | collective-permute-done | bytes 32800 | tf_op jit(solution)/shard_map/ppermute | solution.py:376
  52.0 0.7 %collective-permute-done.16.refs_2_ = f32[8,1024]{1,0:T(8,128)S(1)} collective-permute-done((f32[8,1024]{1,0:T(8,128)S(1)}, f32[8,1024]{1,0:T(8,128)S(1)}, u32[]{:S(2)}, u32[]{:S(2)}) %collective-permute-start.16) | collective-permute-done | bytes 32800 | tf_op jit(solution)/shard_map/ppermute | solution.py:376
  52.7 0.8 %collective-permute-done.17.refs_1_ = f32[8,1024]{1,0:T(8,128)S(1)} collective-permute-done((f32[8,1024]{1,0:T(8,128)S(1)}, f32[8,1024]{1,0:T(8,128)S(1)}, u32[]{:S(2)}, u32[]{:S(2)}) %collective-permute-start.17) | collective-permute-done | bytes 32800 | tf_op jit(solution)/shard_map/ppermute | solution.py:376
  53.5 0.7 %assemble.1 = f32[8,4096]{1,0:T(8,128)} custom-call(f32[8,1024]{1,0:T(8,128)S(1)} %get-tuple-element.69.refs_0_, f32[8,1024]{1,0:T(8,128)S(1)} %collective-permute-done.17.refs_1_, f32[8,1024]{1,0:T(8,128)S(1)} %collective-permute-done.16.refs_2_, f32[8,1024]{1,0:T(8,128)S(1)} %collective-permute-done.15.refs_3_), custom_call_target="tpu_custom_call" | custom-call | tf_op jit(solution)/shard_map/assemble/pallas_call | solution.py:360
  (5 shorter events, 0.1 us)
Async XLA Ops:
  6.2 1.9 %collective-permute-start = (f32[512,128]{1,0:T(8,128)S(1)}, f32[512,128]{1,0:T(8,128)S(1)}, u32[]{:S(2)}, u32[]{:S(2)}) collective-permute-start(f32[512,128]{1,0:T(8,128)S(1)} %get-tuple-element.39.refs_0_), channel_id=1, source_target_pairs={{0,1},{1,0},{2,3},{3,2},{4,5},{5,4},{6,7},{7,6},{8,9},{9,8},{10,11... | collective-permute-start | bytes 786440 | tf_op jit(solution)/shard_map/ppermute | solution.py:383
  8.0 1.4 %collective-permute-start.1 = (f32[256,128]{1,0:T(8,128)S(1)}, f32[256,128]{1,0:T(8,128)S(1)}, u32[]{:S(2)}, u32[]{:S(2)}) collective-permute-start(f32[256,128]{1,0:T(8,128)S(1)} %last_sketch.1.refs_0_), channel_id=1, source_target_pairs={{0,1},{1,0},{2,3},{3,2},{4,5},{5,4},{6,7},{7,6},{8,9},{9,8},{10,11... | collective-permute-start | bytes 393224 | tf_op jit(solution)/shard_map/ppermute | solution.py:383
  10.1 16.9 %collective-permute-start.8 = (f32[128,1024]{1,0:T(8,128)S(1)}, f32[128,1024]{1,0:T(8,128)S(1)}, u32[]{:S(2)}, u32[]{:S(2)}) collective-permute-start(f32[128,1024]{1,0:T(8,128)S(1)} %get-tuple-element.50), channel_id=1, source_target_pairs={{0,2},{2,0},{4,6},{6,4},{8,10},{10,8},{12,14},{14,12},{16,18},{18,... | collective-permute-start | bytes 1572872 | tf_op jit(solution)/shard_map/ppermute | solution.py:376
  13.0 14.9 %collective-permute-start.10 = (f32[128,1024]{1,0:T(8,128)S(1)}, f32[128,1024]{1,0:T(8,128)S(1)}, u32[]{:S(2)}, u32[]{:S(2)}) collective-permute-start(f32[128,1024]{1,0:T(8,128)S(1)} %get-tuple-element.51), channel_id=1, source_target_pairs={{0,4},{2,6},{4,0},{6,2},{8,12},{10,14},{12,8},{14,10},{16,20},{18,... | collective-permute-start | bytes 1572872 | tf_op jit(solution)/shard_map/ppermute | solution.py:376
  14.9 6.2 %collective-permute-start.4 = (f32[72,128]{1,0:T(8,128)S(1)}, f32[72,128]{1,0:T(8,128)S(1)}, u32[]{:S(2)}, u32[]{:S(2)}) collective-permute-start(f32[72,128]{1,0:T(8,128)S(1)} %gram.1), channel_id=1, source_target_pairs={{0,24},{2,26},{4,28},{6,30},{8,16},{10,18},{12,20},{14,22},{16,8},... | collective-permute-start | bytes 110600 | tf_op jit(solution)/shard_map/ppermute | solution.py:376
  18.6 4.9 %collective-permute-start.3 = (f32[72,128]{1,0:T(8,128)S(1)}, f32[72,128]{1,0:T(8,128)S(1)}, u32[]{:S(2)}, u32[]{:S(2)}) collective-permute-start(f32[72,128]{1,0:T(8,128)S(1)} %gram.1), channel_id=1, source_target_pairs={{0,16},{2,18},{4,20},{6,22},{8,24},{10,26},{12,28},{14,30},{16,0},... | collective-permute-start | bytes 110600 | tf_op jit(solution)/shard_map/ppermute | solution.py:376
  18.6 4.9 %collective-permute-start.2 = (f32[72,128]{1,0:T(8,128)S(1)}, f32[72,128]{1,0:T(8,128)S(1)}, u32[]{:S(2)}, u32[]{:S(2)}) collective-permute-start(f32[72,128]{1,0:T(8,128)S(1)} %gram.1), channel_id=1, source_target_pairs={{0,8},{2,10},{4,12},{6,14},{8,0},{10,2},{12,4},{14,6},{16,24},{18,... | collective-permute-start | bytes 110600 | tf_op jit(solution)/shard_map/ppermute | solution.py:376
  23.5 6.0 %collective-permute-start.7 = (f32[72,128]{1,0:T(8,128)S(1)}, f32[72,128]{1,0:T(8,128)S(1)}, u32[]{:S(2)}, u32[]{:S(2)}) collective-permute-start(f32[72,128]{1,0:T(8,128)S(1)} %add_add_fusion.1), channel_id=1, source_target_pairs={{0,6},{2,4},{4,2},{6,0},{8,14},{10,12},{12,10},{14,8},{16,22},{18,... | collective-permute-start | bytes 110600 | tf_op jit(solution)/shard_map/ppermute | solution.py:376
  24.0 5.5 %collective-permute-start.6 = (f32[72,128]{1,0:T(8,128)S(1)}, f32[72,128]{1,0:T(8,128)S(1)}, u32[]{:S(2)}, u32[]{:S(2)}) collective-permute-start(f32[72,128]{1,0:T(8,128)S(1)} %add_add_fusion.1), channel_id=1, source_target_pairs={{0,4},{2,6},{4,0},{6,2},{8,12},{10,14},{12,8},{14,10},{16,20},{18,... | collective-permute-start | bytes 110600 | tf_op jit(solution)/shard_map/ppermute | solution.py:376
  25.5 4.4 %collective-permute-start.5 = (f32[72,128]{1,0:T(8,128)S(1)}, f32[72,128]{1,0:T(8,128)S(1)}, u32[]{:S(2)}, u32[]{:S(2)}) collective-permute-start(f32[72,128]{1,0:T(8,128)S(1)} %add_add_fusion.1), channel_id=1, source_target_pairs={{0,2},{2,0},{4,6},{6,4},{8,10},{10,8},{12,14},{14,12},{16,18},{18,... | collective-permute-start | bytes 110600 | tf_op jit(solution)/shard_map/ppermute | solution.py:376
  27.1 8.3 %collective-permute-start.9 = (f32[128,512]{1,0:T(8,128)S(1)}, f32[128,512]{1,0:T(8,128)S(1)}, u32[]{:S(2)}, u32[]{:S(2)}) collective-permute-start(f32[128,512]{1,0:T(8,128)S(1)} %onward.2), channel_id=1, source_target_pairs={{0,4},{2,6},{4,0},{6,2},{8,12},{10,14},{12,8},{14,10},{16,20},{18,... | collective-permute-start | bytes 786440 | tf_op jit(solution)/shard_map/ppermute | solution.py:376
  28.0 7.4 %collective-permute-start.11 = (f32[128,512]{1,0:T(8,128)S(1)}, f32[128,512]{1,0:T(8,128)S(1)}, u32[]{:S(2)}, u32[]{:S(2)}) collective-permute-start(f32[128,512]{1,0:T(8,128)S(1)} %onward.3), channel_id=1, source_target_pairs={{0,2},{2,0},{4,6},{6,4},{8,10},{10,8},{12,14},{14,12},{16,18},{18,... | collective-permute-start | bytes 786440 | tf_op jit(solution)/shard_map/ppermute | solution.py:376
  35.7 11.1 %collective-permute-start.12 = (f32[32,1024]{1,0:T(8,128)S(1)}, f32[32,1024]{1,0:T(8,128)S(1)}, u32[]{:S(2)}, u32[]{:S(2)}) collective-permute-start(f32[32,1024]{1,0:T(8,128)S(1)} %get-tuple-element.59), channel_id=1, source_target_pairs={{0,16},{2,18},{4,20},{6,22},{8,24},{10,26},{12,28},{14,30},{16,0},... | collective-permute-start | bytes 393224 | tf_op jit(solution)/shard_map/ppermute | solution.py:376
  38.0 8.8 %collective-permute-start.13 = (f32[32,1024]{1,0:T(8,128)S(1)}, f32[32,1024]{1,0:T(8,128)S(1)}, u32[]{:S(2)}, u32[]{:S(2)}) collective-permute-start(f32[32,1024]{1,0:T(8,128)S(1)} %get-tuple-element.60), channel_id=1, source_target_pairs={{0,24},{2,26},{4,28},{6,30},{8,16},{10,18},{12,20},{14,22},{16,8},... | collective-permute-start | bytes 393224 | tf_op jit(solution)/shard_map/ppermute | solution.py:376
  39.4 7.7 %collective-permute-start.14 = (f32[32,1024]{1,0:T(8,128)S(1)}, f32[32,1024]{1,0:T(8,128)S(1)}, u32[]{:S(2)}, u32[]{:S(2)}) collective-permute-start(f32[32,1024]{1,0:T(8,128)S(1)} %get-tuple-element.61), channel_id=1, source_target_pairs={{0,8},{2,10},{4,12},{6,14},{8,0},{10,2},{12,4},{14,6},{16,24},{18,... | collective-permute-start | bytes 393224 | tf_op jit(solution)/shard_map/ppermute | solution.py:376
  47.1 4.9 %collective-permute-start.15 = (f32[8,1024]{1,0:T(8,128)S(1)}, f32[8,1024]{1,0:T(8,128)S(1)}, u32[]{:S(2)}, u32[]{:S(2)}) collective-permute-start(f32[8,1024]{1,0:T(8,128)S(1)} %get-tuple-element.70), channel_id=1, source_target_pairs={{0,6},{2,4},{4,2},{6,0},{8,14},{10,12},{12,10},{14,8},{16,22},{18,... | collective-permute-start | bytes 98312 | tf_op jit(solution)/shard_map/ppermute | solution.py:376
  48.8 3.9 %collective-permute-start.16 = (f32[8,1024]{1,0:T(8,128)S(1)}, f32[8,1024]{1,0:T(8,128)S(1)}, u32[]{:S(2)}, u32[]{:S(2)}) collective-permute-start(f32[8,1024]{1,0:T(8,128)S(1)} %get-tuple-element.71), channel_id=1, source_target_pairs={{0,4},{2,6},{4,0},{6,2},{8,12},{10,14},{12,8},{14,10},{16,20},{18,... | collective-permute-start | bytes 98312 | tf_op jit(solution)/shard_map/ppermute | solution.py:376
  49.5 3.9 %collective-permute-start.17 = (f32[8,1024]{1,0:T(8,128)S(1)}, f32[8,1024]{1,0:T(8,128)S(1)}, u32[]{:S(2)}, u32[]{:S(2)}) collective-permute-start(f32[8,1024]{1,0:T(8,128)S(1)} %get-tuple-element.72), channel_id=1, source_target_pairs={{0,2},{2,0},{4,6},{6,4},{8,10},{10,8},{12,14},{14,12},{16,18},{18,... | collective-permute-start | bytes 98312 | tf_op jit(solution)/shard_map/ppermute | solution.py:376
